TPU v7x, 32 devices: a whole 2x2x4 slice. The times are simulated.
32 devices in a mesh: groups: 2 (over x), orb: 16 (over z, y, core).
Axes of the slice: x: 2, y: 2, z: 4, core: 2. Of those that a mesh axis runs over, the one named last changes fastest.
Arguments:
- pair_list: int32 [2048, 2], P(('groups', 'orb')), parts along dimension 0, may hold values from 0 to 511, as said below
- orbital_slot: int32 [1024], P('groups'), parts along dimension 0, may hold values from 0 to 511, as said below
- blocks: bfloat16 [1024, 512, 128], P(('groups', 'orb')), parts along dimension 0, may hold values from -0.59765625 to 0.59765625
- transforms: bfloat16 [1024, 128, 128], P(('groups', 'orb')), parts along dimension 0, may hold values from -0.5 to 0.5
- domain: int32 [1024, 128], P(('groups', 'orb')), parts along dimension 0, may hold values from 0 to 2047
- eps_virt: float32 [4096], P('groups'), parts along dimension 0, may hold values from 0.2 to 2.5
- eps_occ: float32 [1024], P('groups'), parts along dimension 0, may hold values from -1.5 to -0.3
- offsets: int32 [1024], P('groups'), parts along dimension 0, may hold values from 0 to 3
Outputs:
- pair_energy: float32 [2048], P(('groups', 'orb')), parts along dimension 0
- density: float32 [1024, 128, 128], P(('groups', 'orb')), parts along dimension 0
There are 2 independent parts, one for each index of `groups`. A program takes and returns all parts, laid end to end along the dimension named above; each array names one. Nothing has to cross between parts.
Inputs may be any that keep to these rules, and one draw needn't show every extreme that they name: `pair_list`: the 64 pairs of each aligned block (one device's pairs) have their first orbital stored in that block's device, slots 32 * d to 32 * (d + 1) - 1 for block d. Within one block, the pairs whose second orbital is stored on one device are at most 4, and they all name the same second orbital; this most is reached. No pair names one orbital twice. `orbital_slot`: A permutation of the orbital ids.
All inputs are finite; a program needn't handle non-finite values.
Results may differ from a plain program's by a relative error of at most 0.0022.
Values may be sent and summed in bfloat16 or wider, within the bound.
No kernel may reach another device: no remote copies, remote signals or barrier semaphores. Data moves between devices by JAX's collectives and lax.ppermute only.
A program may use at most 128 MiB of HBM per device.

v0:
```python
import jax
import jax.numpy as jnp
from jax import lax
from jax.sharding import PartitionSpec as P

AUXBLK = 128


full_precision = lax.Precision.HIGHEST


def local_sums(targets, row_count, values):
    picker = (targets[None, :] == jnp.arange(row_count, dtype=jnp.int32)[:, None]).astype(
        jnp.float32
    )
    flattened = values.reshape(values.shape[0], -1)
    summed = jnp.dot(
        picker, flattened, precision=full_precision, preferred_element_type=jnp.float32
    )
    return summed.reshape((row_count,) + values.shape[1:])


def local(pair_list, orbital_slot, blocks, transforms, domain, eps_virt, eps_occ, offsets):
    owners = lax.axis_size("orb")
    device_index = lax.axis_index("orb")
    orb_dev, fit_rows, domain_width = blocks.shape
    pair_dev = pair_list.shape[0]
    block_count = fit_rows // AUXBLK
    slot_i = orbital_slot[pair_list[:, 0]]
    slot_j = orbital_slot[pair_list[:, 1]]
    local_i = slot_i - device_index * orb_dev
    owner_j = slot_j // orb_dev
    local_j = slot_j % orb_dev
    rotated = jnp.einsum(
        "srv,svw->srw", blocks, transforms, preferred_element_type=jnp.float32
    ).astype(jnp.bfloat16)
    dom_energy = eps_virt[domain].astype(jnp.bfloat16)
    pair_order = jnp.arange(pair_dev, dtype=jnp.int32)
    slot_cap = -(-pair_dev // owners)
    earlier = (owner_j[None, :] == owner_j[:, None]) & (pair_order[None, :] < pair_order[:, None])
    held_slot = owner_j * slot_cap + jnp.sum(earlier, axis=1)
    wanted = (
        jnp.full((owners * slot_cap,), -1, jnp.int32)
        .at[held_slot]
        .set(local_j)
        .reshape(owners, slot_cap)
    )
    asked_for = lax.all_to_all(wanted, "orb", split_axis=0, concat_axis=0, tiled=True)
    is_valid = (asked_for >= 0).astype(jnp.bfloat16)
    picked = jnp.maximum(asked_for, 0)
    outgoing = rotated[picked] * is_valid[:, :, None, None]
    energies = dom_energy[picked]
    incoming, far_energy = (
        lax.all_to_all(outgoing, "orb", split_axis=0, concat_axis=0, tiled=True),
        lax.all_to_all(energies, "orb", split_axis=0, concat_axis=0, tiled=True),
    )
    incoming = incoming.reshape((owners * slot_cap, fit_rows, domain_width))
    far_energy = far_energy.reshape((owners * slot_cap, domain_width))
    block_shift = offsets[slot_i] - offsets[slot_j]
    source = jnp.arange(block_count, dtype=jnp.int32)[None, :] + block_shift[:, None]
    inside = ((source >= 0) & (source < block_count)).astype(jnp.bfloat16)
    row_index = held_slot[:, None] * block_count + jnp.clip(source, 0, block_count - 1)
    pieces = incoming.reshape((-1, AUXBLK, domain_width))[row_index] * inside[:, :, None, None]
    own_rows = rotated[local_i].reshape((pair_dev, block_count, AUXBLK, domain_width))
    coupling = jnp.einsum("pkrv,pkrw->pvw", own_rows, pieces, preferred_element_type=jnp.float32)
    denominator = (
        dom_energy[local_i].astype(jnp.float32)[:, :, None]
        + far_energy[held_slot].astype(jnp.float32)[:, None, :]
        - (eps_occ[slot_i] + eps_occ[slot_j])[:, None, None]
    )
    amplitude = coupling / denominator
    pair_energy = -jnp.sum(coupling * amplitude, axis=(1, 2)) / domain_width
    amp_half = amplitude.astype(jnp.bfloat16)
    left_density = jnp.einsum(
        "pab,pcb->pac", amp_half, amp_half, preferred_element_type=jnp.float32
    )
    inner_sum = local_sums(local_i, orb_dev, left_density)
    right_density = jnp.einsum(
        "pab,pac->pbc", amp_half, amp_half, preferred_element_type=jnp.float32
    )
    sent_back = (
        jnp.zeros((owners * slot_cap, domain_width, domain_width), jnp.float32)
        .at[held_slot]
        .set(right_density)
    )
    sent_back = sent_back.reshape((owners, slot_cap, domain_width, domain_width))
    came_back = lax.all_to_all(sent_back, "orb", split_axis=0, concat_axis=0, tiled=True)
    came_back = came_back.reshape((owners * slot_cap, domain_width, domain_width))
    inner_sum = inner_sum + local_sums(asked_for.reshape(-1), orb_dev, came_back)
    turned = transforms.astype(jnp.float32)
    density = jnp.einsum("sab,sbc->sac", turned, inner_sum, precision=full_precision)
    density = jnp.einsum("sac,sdc->sad", density, turned, precision=full_precision)
    return (pair_energy, density)


def solution(mesh):
    in_specs = (
        P(("groups", "orb"), None),
        P("groups"),
        P(("groups", "orb"), None, None),
        P(("groups", "orb"), None, None),
        P(("groups", "orb"), None),
        P("groups"),
        P("groups"),
        P("groups"),
    )
    out_specs = (P(("groups", "orb")), P(("groups", "orb"), None, None))
    return jax.shard_map(local, mesh=mesh, in_specs=in_specs, out_specs=out_specs, check_vma=False)
```

profile of v0, /device:TPU:13, one launch (start us, length us, event | category | flops | bytes accessed | tf_op | source)
XLA Modules:
  0.0 402.4 jit_solution(16610695200208484276)
XLA Ops:
  0.6 0.0 copy-start
  0.6 0.8 fusion.33
  1.4 1.5 gather_fusion.2
  2.9 0.2 convert_reduce_fusion
  3.1 0.8 scatter_custom_fusion
  3.9 0.7 all_to_all.15
  4.6 6.6 %all-to-all-start = ((s32[16,1,4]{2,1,0:T(1,128)}), s32[16,1,4]{2,1,0:T(1,128)S(1)}, u32[]{:S(2)}, u32[]{:S(2)}) async-start(s32[16,1,4]{2,1,0:T(1,128)} %bitcast.8), calls=%async_computation | async-start | bytes 16384 | tf_op jit(solution)/shard_map/all_to_all | solution.py:48
  11.2 0.0 copy-done
  11.2 0.0 copy-start.6
  11.2 0.0 copy-start.1
  11.2 5.4 %convolution_convert_fusion = bf16[32,512,128]{2,1,0:T(8,128)(2,1)} fusion(bf16[32,512,128]{2,1,0:T(8,128)(2,1)} %param.10, bf16[32,128,128]{2,1,0:T(8,128)(2,1)S(1)} %copy-done), kind=kOutput, calls=%fused_computation.31 | convolution fusion | flops 538968064 | bytes 9437184 | tf_op jit(solution)/shard_map/srv,svw->srw/dot_general | solution.py:34
  16.6 0.0 copy-done.6
  16.6 0.0 copy-done.1
  16.6 22.7 %gather_fusion.7 = bf16[4096]{0:T(1024)(128)(2,1)S(1)} fusion(f32[2048]{0:T(1024)S(1)} %copy-done.1, s32[4096]{0:T(1024)S(1)} %fusion.18), kind=kCustom, calls=%fused_computation.7 | custom fusion | bytes 32768 | tf_op jit(solution)/shard_map/gather | solution.py:37
  39.4 0.0 all-to-all-done
  39.4 0.1 copy.44
  39.5 0.1 copy.45
  39.6 0.1 reshape.320
  39.7 0.1 copy.47
  39.8 7.7 %gather_fusion.3 = bf16[64,512,128]{2,1,0:T(8,128)(2,1)} fusion(bf16[32,512,128]{2,1,0:T(8,128)(2,1)} %convolution_convert_fusion, s32[1024]{0:T(1024)S(1)} %pad_clamp_fusion.4), kind=kCustom, calls=%fused_computation.3 | custom fusion | bytes 16777472 | tf_op jit(solution)/shard_map/gather | solution.py:51
  47.5 1.2 gather_fusion.9
  48.7 6.0 %all-to-all-start.2 = ((bf16[16,4,128]{2,1,0:T(4,128)(2,1)}), bf16[16,4,128]{2,1,0:T(4,128)(2,1)S(1)}, u32[]{:S(2)}, u32[]{:S(2)}) async-start(bf16[16,4,128]{2,1,0:T(4,128)(2,1)} %bitcast.19), calls=%async_computation.2 | async-start | bytes 32768 | tf_op jit(solution)/shard_map/all_to_all | solution.py:55
  54.7 7.2 %broadcast_multiply_fusion = bf16[16,4,512,128]{3,2,1,0:T(8,128)(2,1)} fusion(bf16[16,4,512,128]{3,2,1,0:T(8,128)(2,1)} %bitcast.109, bf16[16,4]{1,0:T(8,128)(2,1)S(1)} %copy.47), kind=kLoop, calls=%fused_computation.29 | loop fusion | flops 4194304 | bytes 16777344 | tf_op jit(solution)/shard_map/mul | solution.py:51
  62.0 0.0 copy-start.2
  62.0 0.0 copy-start.3
  62.0 0.0 copy-start.4
  62.0 0.0 all-to-all-done.2
  62.0 6.2 %all-to-all-start.1 = ((bf16[16,4,512,128]{3,2,1,0:T(8,128)(2,1)}), bf16[16,4,512,128]{3,2,1,0:T(8,128)(2,1)}, u32[]{:S(2)}, u32[]{:S(2)}) async-start(bf16[16,4,512,128]{3,2,1,0:T(8,128)(2,1)} %broadcast_multiply_fusion), calls=%async_computation.1 | async-start | bytes 16777216 | tf_op jit(solution)/shard_map/all_to_all | solution.py:54
  68.1 0.0 copy-done.2
  68.1 0.8 gather_fusion
  68.9 0.0 copy-done.3
  69.0 0.8 gather_fusion.5
  69.8 0.8 gather_fusion.4
  70.6 0.0 copy-done.4
  70.6 0.8 gather_fusion.12
  71.4 0.8 gather_fusion.11
  72.2 7.7 %gather_fusion.1 = bf16[64,512,128]{2,1,0:T(8,128)(2,1)} fusion(bf16[32,512,128]{2,1,0:T(8,128)(2,1)} %convolution_convert_fusion, s32[1024]{0:T(1024)S(1)} %pad_clamp_fusion.6), kind=kCustom, calls=%fused_computation.1 | custom fusion | bytes 16777472 | tf_op jit(solution)/shard_map/gather | solution.py:64
  79.9 0.6 gather_fusion.8
  80.5 0.1 compare_select_fusion
  80.6 0.1 reshape.344
  80.8 0.1 copy.48
  80.9 0.6 gather_fusion.10
  81.6 168.9 %all-to-all-done.1 = bf16[16,4,512,128]{3,2,1,0:T(8,128)(2,1)} async-done(((bf16[16,4,512,128]{3,2,1,0:T(8,128)(2,1)}), bf16[16,4,512,128]{3,2,1,0:T(8,128)(2,1)}, u32[]{:S(2)}, u32[]{:S(2)}) %all-to-all-start.1) | async-done | bytes 8388640 | tf_op jit(solution)/shard_map/all_to_all | solution.py:54
  250.5 12.0 %gather_fusion.6 = bf16[256,128,128]{2,1,0:T(8,128)(2,1)} fusion(bf16[256,128,128]{2,1,0:T(8,128)(2,1)} %bitcast.11, s32[1024]{0:T(1024)S(1)} %pad_clamp_fusion.1), kind=kCustom, calls=%fused_computation.6 | custom fusion | bytes 16778240 | tf_op jit(solution)/shard_map/gather | solution.py:63
  262.5 8.5 %fusion.10 = (bf16[64,128,128]{2,1,0:T(8,128)(2,1)S(1)}, f32[64]{0:T(128)S(1)}) fusion(f32[64]{0:T(128)S(1)} %add.205, f32[64,128]{1,0:T(8,128)S(1)} %convert_element_type.53, f32[64,128]{1,0:T(8,128)S(1)} %convert_element_type.52, bf16[64,4,128,128]{3,2,1,0:T(8,128)(2,1)} %bitcast.113, bf16[64,4,128,128]{3,2,1,0:T(8,128)(2,1)} %bitcast.114, ...), kind=kOutput, calls=%fused_computation.30 | convolution fusion | flops 1084227584 | bytes 18940928 | tf_op jit(solution)/shard_map/pkrv,pkrw->pvw/dot_general | solution.py:65
  271.0 2.8 fusion.39
  273.8 2.5 broadcast_in_dim.8
  276.3 12.0 %scatter_fusion = f32[64,128,128]{2,1,0:T(8,128)} fusion(f32[64,128,128]{2,1,0:T(8,128)} %broadcast_in_dim.8, s32[64]{0:T(128)S(1)} %get-tuple-element.7, f32[64,128,128]{2,1,0:T(8,128)} %fusion.39), kind=kCustom, calls=%fused_computation.14 | custom fusion | bytes 12583168 | tf_op jit(solution)/shard_map/scatter | solution.py:84
  288.3 5.0 %all-to-all-start.3 = ((f32[16,4,128,128]{3,2,1,0:T(8,128)}), f32[16,4,128,128]{3,2,1,0:T(8,128)}, u32[]{:S(2)}, u32[]{:S(2)}) async-start(f32[16,4,128,128]{3,2,1,0:T(8,128)} %bitcast.108), calls=%async_computation.3 | async-start | bytes 8388608 | tf_op jit(solution)/shard_map/all_to_all | solution.py:87
  293.3 0.5 broadcast.408
  293.8 0.7 reduce.3
  294.5 0.1 eq.49
  294.5 0.5 negate_multiply_fusion
  295.1 3.5 fusion.38
  298.6 87.1 %all-to-all-done.3 = f32[16,4,128,128]{3,2,1,0:T(8,128)} async-done(((f32[16,4,128,128]{3,2,1,0:T(8,128)}), f32[16,4,128,128]{3,2,1,0:T(8,128)}, u32[]{:S(2)}, u32[]{:S(2)}) %all-to-all-start.3) | async-done | bytes 4194336 | tf_op jit(solution)/shard_map/all_to_all | solution.py:87
  385.7 0.0 copy-start.5
  385.7 6.2 %fusion.2 = f32[32,128,128]{2,0,1:T(8,128)S(1)} fusion(s32[64]{0:T(128)S(1)} %eq.49, f32[8,8,128,128]{3,2,1,0:T(8,128)} %bitcast.35), kind=kOutput, calls=%fused_computation.19 | convolution fusion | flops 402655232 | bytes 6291712 | tf_op jit(solution)/shard_map/dot_general | solution.py:17
  392.0 0.0 copy-done.5
  392.0 4.2 %fusion.13 = f32[32,128,128]{2,0,1:T(8,128)S(1)} fusion(f32[32,128,128]{2,0,1:T(8,128)S(1)} %fusion.2, s32[64]{0:T(128)S(1)} %broadcast_subtract_fusion, f32[8,8,128,128]{3,2,1,0:T(8,128)S(1)} %bitcast.110), kind=kOutput, calls=%fused_computation.34 | convolution fusion | flops 403179520 | bytes 8388864 | tf_op jit(solution)/shard_map/dot_general | solution.py:17
  396.1 2.6 fusion.11
  398.7 3.6 fusion.40
  (20 shorter events, 0.1 us)
Async XLA Ops:
  0.6 10.5 %copy-start = (bf16[32,128,128]{2,1,0:T(8,128)(2,1)S(1)}, bf16[32,128,128]{2,1,0:T(8,128)(2,1)}, u32[]{:S(2)}) copy-start(bf16[32,128,128]{2,1,0:T(8,128)(2,1)} %param.11) | copy-start | bytes 3145732
  4.6 34.8 %all-to-all-start = ((s32[16,1,4]{2,1,0:T(1,128)}), s32[16,1,4]{2,1,0:T(1,128)S(1)}, u32[]{:S(2)}, u32[]{:S(2)}) async-start(s32[16,1,4]{2,1,0:T(1,128)} %bitcast.8), calls=%async_computation | async-start | bytes 16384 | tf_op jit(solution)/shard_map/all_to_all | solution.py:48
  11.2 5.4 %copy-start.6 = (s32[32,128]{1,0:T(8,128)S(1)}, s32[32,128]{1,0:T(8,128)}, u32[]{:S(2)}) copy-start(s32[32,128]{1,0:T(8,128)} %param.12) | copy-start | bytes 49156
  11.2 5.4 %copy-start.1 = (f32[2048]{0:T(1024)S(1)}, f32[2048]{0:T(1024)}, u32[]{:S(2)}) copy-start(f32[2048]{0:T(1024)} %param.13) | copy-start | bytes 24580
  48.7 13.3 %all-to-all-start.2 = ((bf16[16,4,128]{2,1,0:T(4,128)(2,1)}), bf16[16,4,128]{2,1,0:T(4,128)(2,1)S(1)}, u32[]{:S(2)}, u32[]{:S(2)}) async-start(bf16[16,4,128]{2,1,0:T(4,128)(2,1)} %bitcast.19), calls=%async_computation.2 | async-start | bytes 32768 | tf_op jit(solution)/shard_map/all_to_all | solution.py:55
  62.0 6.2 %copy-start.2 = (s32[512]{0:T(512)S(1)}, s32[512]{0:T(512)}, u32[]{:S(2)}) copy-start(s32[512]{0:T(512)} %param.9) | copy-start | bytes 6148
  62.0 7.0 %copy-start.3 = (s32[512]{0:T(512)S(1)}, s32[512]{0:T(512)}, u32[]{:S(2)}) copy-start(s32[512]{0:T(512)} %param.15) | copy-start | bytes 6148
  62.0 8.6 %copy-start.4 = (f32[512]{0:T(512)S(1)}, f32[512]{0:T(512)}, u32[]{:S(2)}) copy-start(f32[512]{0:T(512)} %param.14) | copy-start | bytes 6148
  62.0 188.5 %all-to-all-start.1 = ((bf16[16,4,512,128]{3,2,1,0:T(8,128)(2,1)}), bf16[16,4,512,128]{3,2,1,0:T(8,128)(2,1)}, u32[]{:S(2)}, u32[]{:S(2)}) async-start(bf16[16,4,512,128]{3,2,1,0:T(8,128)(2,1)} %broadcast_multiply_fusion), calls=%async_computation.1 | async-start | bytes 16777216 | tf_op jit(solution)/shard_map/all_to_all | solution.py:54
  288.3 97.5 %all-to-all-start.3 = ((f32[16,4,128,128]{3,2,1,0:T(8,128)}), f32[16,4,128,128]{3,2,1,0:T(8,128)}, u32[]{:S(2)}, u32[]{:S(2)}) async-start(f32[16,4,128,128]{3,2,1,0:T(8,128)} %bitcast.108), calls=%async_computation.3 | async-start | bytes 8388608 | tf_op jit(solution)/shard_map/all_to_all | solution.py:87
  385.7 6.2 %copy-start.5 = (f32[64,128,128]{2,1,0:T(8,128)S(1)}, f32[64,128,128]{2,1,0:T(8,128)}, u32[]{:S(2)}) copy-start(f32[64,128,128]{2,1,0:T(8,128)} %fusion.38) | copy-start | bytes 12582916
where the time goes:
time: 403 us; the launch traced here: 402 us
  waiting for transfers between devices  256 us (64%)
  local copies, waits for them, and re-layouts  75.3 us (19%)
  matrix products  36.8 us (9%)
  starting transfers between devices  23.7 us (6%)
  other arithmetic  9.58 us (2%)
    all_to_all x1, waiting for transfers between devices, local(): lax.all_to_all(outgoing, 'orb', split_axis=0, concat_axis=0, tiled=True)  169 us
    all_to_all x1, waiting for transfers between devices, local(): lax.all_to_all(sent_back, 'orb', split_axis=0, concat_axis=0, tiled=True)  87.1 us
    gather x1, local copies, waits for them, and re-layouts, local(): dom_energy = eps_virt[domain].astype(jnp.bfloat16)  22.7 us
    gather x1, local copies, waits for them, and re-layouts, local(): incoming.reshape((-1, AUXBLK, domain_width))[row_index]  12 us
    scatter x1, local copies, waits for them, and re-layouts, local(): sent_back = jnp.zeros((owners * slot_cap, domain_width, domain_width), jn...  12 us
    dot_general x2, matrix products, local_sums(): jnp.dot(picker, flattened, precision=full_precision, preferred_element_ty...  10.4 us
    dot_general x1, matrix products, local(): jnp.einsum('pkrv,pkrw->pvw', own_rows, pieces, preferred_element_type=jnp...  8.5 us
  transfers between devices with their start and end apart: 4, of which 2 were waited for; matrix products, arithmetic and copies ran while one was open for 13% of the time, Pallas kernels for 0%

commit v1 on v0

v1 whole, which is shorter than its diff:
```python
import functools

import jax
import jax.numpy as jnp
from jax import lax
from jax.experimental import pallas as pl
from jax.experimental.pallas import tpu as pltpu
from jax.sharding import PartitionSpec as P

AUXBLK = 128
ENERGY_ROWS = 16
VMEM_LIMIT = 48 * 1024 * 1024

SMEM = functools.partial(pl.BlockSpec, memory_space=pltpu.SMEM)
VMEM = functools.partial(pl.BlockSpec, memory_space=pltpu.VMEM)


def f32_dot(lhs, rhs, dims):
    return lax.dot_general(lhs, rhs, (dims, ((), ())), preferred_element_type=jnp.float32)


def split_dot(lhs, rhs, dims, wide):
    value = (lhs, rhs)[wide]
    high = value.astype(jnp.bfloat16)
    low = (value - high.astype(jnp.float32)).astype(jnp.bfloat16)
    if wide == 0:
        return f32_dot(high, rhs, dims) + f32_dot(low, rhs, dims)
    return f32_dot(lhs, high, dims) + f32_dot(lhs, low, dims)


def plan_kernel(orb_dev, cap, pairs, slots, offsets, eps_occ, wanted, index, first, shift, occupied, seen):
    owners = wanted.shape[0]

    def clear(owner, carry):
        seen[owner] = 0
        return carry

    lax.fori_loop(0, owners, clear, 0)

    def one_pair(pair, carry):
        slot_i = slots[pairs[0, pair]]
        slot_j = slots[pairs[1, pair]]
        owner = lax.div(slot_j, jnp.int32(orb_dev))
        local_j = lax.rem(slot_j, jnp.int32(orb_dev))
        rank = seen[owner]
        seen[owner] = rank + 1
        place = owner * cap + rank
        index[place] = pair
        first[place] = lax.rem(slot_i, jnp.int32(orb_dev))
        shift[place] = offsets[slot_i] - offsets[slot_j]
        occupied[place] = eps_occ[slot_i] + eps_occ[slot_j]
        wanted[owner] = jnp.full(wanted.shape[1:], local_j, jnp.int32)
        return carry

    lax.fori_loop(0, pairs.shape[1], one_pair, 0)


def plan(owners, orb_dev, pair_list, orbital_slot, offsets, eps_occ):
    pair_dev = pair_list.shape[0]
    cap = pair_dev // owners
    sorted_ints = jax.ShapeDtypeStruct((pair_dev,), jnp.int32)
    return pl.pallas_call(
        functools.partial(plan_kernel, orb_dev, cap),
        out_shape=(
            jax.ShapeDtypeStruct((owners, 1, 128), jnp.int32),
            sorted_ints,
            sorted_ints,
            sorted_ints,
            jax.ShapeDtypeStruct((pair_dev,), jnp.float32),
        ),
        in_specs=[SMEM()] * 4,
        out_specs=(VMEM(), SMEM(), SMEM(), SMEM(), SMEM()),
        scratch_shapes=[pltpu.SMEM((owners,), jnp.int32)],
        name="plan",
    )(pair_list.T, orbital_slot, offsets, eps_occ)


def energies_kernel(domain, eps_virt, rows, columns):
    orb_dev, width = domain.shape
    wanted = domain[...]
    line, lane = wanted // 128, wanted % 128
    found = jnp.zeros((orb_dev, width), jnp.float32)
    for k in range(eps_virt.shape[0]):
        spread = jnp.broadcast_to(eps_virt[pl.ds(k, 1), :], (orb_dev, width))
        picked = jnp.take_along_axis(spread, lane, axis=1)
        found = jnp.where(line == k, picked, found)
    found = found.astype(jnp.bfloat16).astype(jnp.float32)
    for s in range(orb_dev):
        row = found[s : s + 1, :]
        rows[s] = row
        columns[s] = jnp.broadcast_to(row, (width, width)).T.astype(jnp.bfloat16)


def domain_energies(domain, eps_virt):
    orb_dev, width = domain.shape
    return pl.pallas_call(
        energies_kernel,
        out_shape=(
            jax.ShapeDtypeStruct((orb_dev, 1, width), jnp.float32),
            jax.ShapeDtypeStruct((orb_dev, width, width), jnp.bfloat16),
        ),
        in_specs=[VMEM()] * 2,
        out_specs=(VMEM(), VMEM()),
        compiler_params=pltpu.CompilerParams(vmem_limit_bytes=VMEM_LIMIT),
        name="domain_energies",
    )(domain, eps_virt.reshape(-1, 128))


def own_kernel(blocks, transforms, turned):
    for s in range(blocks.shape[0]):
        turned[s] = f32_dot(transforms[s], blocks[s], ((0,), (1,))).astype(jnp.bfloat16)


def own_rotated(blocks, transforms, per_step=4):
    orb_dev, fit_rows, width = blocks.shape
    return pl.pallas_call(
        own_kernel,
        grid=(orb_dev // per_step,),
        out_shape=jax.ShapeDtypeStruct((orb_dev, width, fit_rows), jnp.bfloat16),
        in_specs=[
            pl.BlockSpec((per_step, fit_rows, width), lambda g: (g, 0, 0)),
            pl.BlockSpec((per_step, width, width), lambda g: (g, 0, 0)),
        ],
        out_specs=pl.BlockSpec((per_step, width, fit_rows), lambda g: (g, 0, 0)),
        compiler_params=pltpu.CompilerParams(vmem_limit_bytes=VMEM_LIMIT),
        name="own_rotated",
    )(blocks, transforms)


def pack_kernel(per_step, asked, rows, *refs):
    blocks, transforms, message = refs[:per_step], refs[per_step : 2 * per_step], refs[-1]
    fit_rows = blocks[0].shape[1]
    step = pl.program_id(0)
    for k in range(per_step):
        rotated = f32_dot(blocks[k][0], transforms[k][0], ((1,), (0,)))
        message[k, :fit_rows, :] = rotated.astype(jnp.bfloat16)
        energy = rows[asked[step * per_step + k]]
        message[k, fit_rows:, :] = jnp.broadcast_to(energy, (ENERGY_ROWS, energy.shape[1])).astype(
            jnp.bfloat16
        )


def pack_messages(asked, rows, blocks, transforms, per_step=4):
    owners = asked.shape[0]
    orb_dev, fit_rows, width = blocks.shape

    def of_slot(k):
        return lambda g, asked: (asked[g * per_step + k], 0, 0)

    return pl.pallas_call(
        functools.partial(pack_kernel, per_step),
        grid_spec=pltpu.PrefetchScalarGridSpec(
            num_scalar_prefetch=1,
            grid=(owners // per_step,),
            in_specs=[pl.BlockSpec((orb_dev, 1, width), lambda g, asked: (0, 0, 0))]
            + [pl.BlockSpec((1, fit_rows, width), of_slot(k)) for k in range(per_step)]
            + [pl.BlockSpec((1, width, width), of_slot(k)) for k in range(per_step)],
            out_specs=pl.BlockSpec(
                (per_step, fit_rows + ENERGY_ROWS, width), lambda g, asked: (g, 0, 0)
            ),
        ),
        out_shape=jax.ShapeDtypeStruct((owners, fit_rows + ENERGY_ROWS, width), jnp.bfloat16),
        compiler_params=pltpu.CompilerParams(vmem_limit_bytes=VMEM_LIMIT),
        name="pack_messages",
    )(asked, rows, *([blocks] * per_step), *([transforms] * per_step))


def pairs_kernel(cap, first, shift, occupied, message, *refs):
    turned, columns = refs[:cap], refs[cap : 2 * cap]
    half, energy, right, padded = refs[2 * cap :]
    width, fit_rows = turned[0].shape[1:]
    margin = fit_rows - AUXBLK
    step = pl.program_id(0)

    @pl.when(step == 0)
    def _():
        zeros = jnp.zeros((margin, width), jnp.bfloat16)
        padded[:margin, :] = zeros
        padded[margin + fit_rows :, :] = zeros

    padded[margin : margin + fit_rows, :] = message[0, :fit_rows, :]
    far = message[0, fit_rows:, :].astype(jnp.float32)[:1, :]
    for k in range(cap):
        place = step * cap + k
        begin = pl.multiple_of(margin + AUXBLK * shift[place], AUXBLK)
        aligned = padded[pl.ds(begin, fit_rows), :]
        coupling = f32_dot(turned[k][0], aligned, ((1,), (0,)))
        denominator = (columns[k][0].astype(jnp.float32) + far) - occupied[place]
        amplitude = coupling / denominator
        energy[k] = jnp.sum(coupling * amplitude, axis=0, keepdims=True)
        half[k] = amplitude.astype(jnp.bfloat16)
    stacked = half[...].reshape(cap * width, width)
    right[0] = f32_dot(stacked, stacked, ((0,), (0,))).astype(jnp.bfloat16)


def pair_terms(first, shift, occupied, messages, turned, columns):
    owners, rows, width = messages.shape
    pair_dev = first.shape[0]
    cap = pair_dev // owners
    fit_rows = turned.shape[2]

    def of_pair(k):
        return lambda g, first, shift, occupied: (first[g * cap + k], 0, 0)

    def of_step(g, first, shift, occupied):
        return (g, 0, 0)

    return pl.pallas_call(
        functools.partial(pairs_kernel, cap),
        grid_spec=pltpu.PrefetchScalarGridSpec(
            num_scalar_prefetch=3,
            grid=(owners,),
            in_specs=[pl.BlockSpec((1, rows, width), of_step)]
            + [pl.BlockSpec((1, width, fit_rows), of_pair(k)) for k in range(cap)]
            + [pl.BlockSpec((1, width, width), of_pair(k)) for k in range(cap)],
            out_specs=(
                pl.BlockSpec((cap, width, width), of_step),
                pl.BlockSpec((cap, 1, width), of_step),
                pl.BlockSpec((1, width, width), of_step),
            ),
            scratch_shapes=[pltpu.VMEM((3 * fit_rows - 2 * AUXBLK, width), jnp.bfloat16)],
        ),
        out_shape=(
            jax.ShapeDtypeStruct((pair_dev, width, width), jnp.bfloat16),
            jax.ShapeDtypeStruct((pair_dev, 1, width), jnp.float32),
            jax.ShapeDtypeStruct((owners, width, width), jnp.bfloat16),
        ),
        compiler_params=pltpu.CompilerParams(vmem_limit_bytes=VMEM_LIMIT),
        name="pair_terms",
    )(first, shift, occupied, messages, *([turned] * cap), *([columns] * cap))


def left_kernel(index, first, half, energy, inner, pair_energy, scattered):
    width = half.shape[2]
    inner[...] = jnp.zeros_like(inner)

    def one_pair(place, carry):
        amplitude = half[place]
        slot = first[place]
        inner[slot] = inner[slot] + f32_dot(amplitude, amplitude, ((1,), (1,)))
        scattered[index[place]] = energy[place]
        return carry

    lax.fori_loop(0, half.shape[0], one_pair, 0, unroll=4)
    gathered = scattered[...].reshape(half.shape[0], width)
    pair_energy[...] = -jnp.sum(gathered, axis=1, keepdims=True) / width


def left_sums(orb_dev, index, first, half, energy):
    pair_dev, width, _ = half.shape
    return pl.pallas_call(
        left_kernel,
        in_specs=[SMEM(), SMEM(), VMEM(), VMEM()],
        out_specs=(VMEM(), VMEM()),
        out_shape=(
            jax.ShapeDtypeStruct((orb_dev, width, width), jnp.float32),
            jax.ShapeDtypeStruct((pair_dev, 1), jnp.float32),
        ),
        scratch_shapes=[pltpu.VMEM((pair_dev, 1, width), jnp.float32)],
        compiler_params=pltpu.CompilerParams(vmem_limit_bytes=VMEM_LIMIT),
        name="left_sums",
    )(index, first, half, energy)


def density_kernel(asked, inner, right, transforms, density):
    orb_dev = inner.shape[0]
    density[...] = inner[...]

    def one_message(device, carry):
        slot = asked[device]
        density[slot] = density[slot] + right[device].astype(jnp.float32)
        return carry

    lax.fori_loop(0, right.shape[0], one_message, 0)

    def one_slot(slot, carry):
        turn = transforms[slot]
        half_way = split_dot(turn, density[slot], ((1,), (0,)), 1)
        density[slot] = split_dot(half_way, turn, ((1,), (1,)), 0)
        return carry

    lax.fori_loop(0, orb_dev, one_slot, 0, unroll=4)


def final_density(asked, inner, right, transforms):
    return pl.pallas_call(
        density_kernel,
        in_specs=[SMEM(), VMEM(), VMEM(), VMEM()],
        out_specs=VMEM(),
        out_shape=jax.ShapeDtypeStruct(inner.shape, jnp.float32),
        compiler_params=pltpu.CompilerParams(vmem_limit_bytes=VMEM_LIMIT),
        name="final_density",
    )(asked, inner, right, transforms)


def exchange(messages):
    return lax.all_to_all(messages, "orb", split_axis=0, concat_axis=0, tiled=True)


def local(pair_list, orbital_slot, blocks, transforms, domain, eps_virt, eps_occ, offsets):
    owners = lax.axis_size("orb")
    orb_dev = blocks.shape[0]
    wanted, index, first, shift, occupied = plan(
        owners, orb_dev, pair_list, orbital_slot, offsets, eps_occ
    )
    asked = exchange(wanted)[:, 0, 0]
    rows, columns = domain_energies(domain, eps_virt)
    turned = own_rotated(blocks, transforms)
    incoming = exchange(pack_messages(asked, rows, blocks, transforms))
    half, energy, right = pair_terms(first, shift, occupied, incoming, turned, columns)
    came_back = exchange(right)
    inner, pair_energy = left_sums(orb_dev, index, first, half, energy)
    density = final_density(asked, inner, came_back, transforms)
    return (pair_energy.reshape(-1), density)


def solution(mesh):
    in_specs = (
        P(("groups", "orb"), None),
        P("groups"),
        P(("groups", "orb"), None, None),
        P(("groups", "orb"), None, None),
        P(("groups", "orb"), None),
        P("groups"),
        P("groups"),
        P("groups"),
    )
    out_specs = (P(("groups", "orb")), P(("groups", "orb"), None, None))
    return jax.shard_map(local, mesh=mesh, in_specs=in_specs, out_specs=out_specs, check_vma=False)
```

time: 403 us -> 122 us (0.30)
  the two profiles are of different devices: /device:TPU:13 before, /device:TPU:0 now
where the time goes in v1:
time: 122 us; the launch traced here: 121 us
  waiting for transfers between devices  46.7 us (38%)
  Pallas kernels  40.1 us (33%)
  starting transfers between devices  23.3 us (19%)
  local copies, waits for them, and re-layouts  9.29 us (8%)
    all_to_all x3, waiting for transfers between devices, exchange(): lax.all_to_all(messages, 'orb', split_axis=0, concat_axis=0, tiled=True)  46.7 us
    all_to_all x3, starting transfers between devices, exchange(): lax.all_to_all(messages, 'orb', split_axis=0, concat_axis=0, tiled=True)  23.3 us
    pallas_call x1, Pallas kernels, pair_terms(): pl.pallas_call(functools.partial(pairs_kernel, cap), grid_spec=pltpu.Pref...  15.5 us
    unnamed x24, local copies, waits for them, and re-layouts  8.91 us
    pallas_call x1, Pallas kernels, final_density(): pl.pallas_call(density_kernel, in_specs=[SMEM(), VMEM(), VMEM(), VMEM()],...  7.25 us
    pallas_call x1, Pallas kernels, own_rotated(): pl.pallas_call(own_kernel, grid=(orb_dev // per_step,), out_shape=jax.Sha...  5.95 us
    pallas_call x1, Pallas kernels, left_sums(): pl.pallas_call(left_kernel, in_specs=[SMEM(), SMEM(), VMEM(), VMEM()], ou...  4.26 us
    pallas_call x1, Pallas kernels, pack_messages(): pl.pallas_call(functools.partial(pack_kernel, per_step), grid_spec=pltpu....  3.76 us
  transfers between devices with their start and end apart: 3, of which 3 were waited for; matrix products, arithmetic and copies ran while one was open for 1% of the time, Pallas kernels for 9%

profile of v1, /device:TPU:0, one launch (start us, length us, event | category | flops | bytes accessed | tf_op | source)
XLA Modules:
  0.0 120.9 jit_solution(11333388568080011757)
XLA Ops:
  0.6 2.9 %plan.1 = (s32[16,1,128]{2,1,0:T(1,128)}, s32[64]{0:T(128)}, s32[64]{0:T(128)}, s32[64]{0:T(128)}, f32[64]{0:T(128)}) custom-call(s32[2,64]{1,0:T(2,128)} %bitcast.3, s32[512]{0:T(512)} %slots.1, s32[512]{0:T(512)} %offsets.1, f32[512]{0:T(512)} %eps_occ.1), custom_call_target="tpu_custom_call" | custom-call | tf_op jit(solution)/shard_map/plan/pallas_call | solution.py:62
  3.6 7.4 %all-to-all-start = ((s32[16,1,128]{2,1,0:T(1,128)}), s32[16,1,128]{2,1,0:T(1,128)S(1)}, u32[]{:S(2)}, u32[]{:S(2)}) async-start(s32[16,1,128]{2,1,0:T(1,128)} %get-tuple-element.18), calls=%async_computation | async-start | bytes 16384 | tf_op jit(solution)/shard_map/all_to_all | solution.py:297
  11.0 0.0 copy-start.6
  11.0 0.7 copy-done.6
  11.7 0.0 copy-start.7
  11.7 0.7 copy-done.7
  12.4 0.5 domain_energies.1
  12.9 4.4 %all-to-all-done = s32[16,1,128]{2,1,0:T(1,128)S(1)} async-done(((s32[16,1,128]{2,1,0:T(1,128)}), s32[16,1,128]{2,1,0:T(1,128)S(1)}, u32[]{:S(2)}, u32[]{:S(2)}) %all-to-all-start) | async-done | bytes 8224 | tf_op jit(solution)/shard_map/all_to_all | solution.py:297
  17.3 0.4 slice_reduce_fusion.asked
  17.7 0.0 copy-start.1
  17.7 1.2 %copy-done.1 = bf16[32,128,128]{2,1,0:T(8,128)(2,1)S(1)} copy-done((bf16[32,128,128]{2,1,0:T(8,128)(2,1)S(1)}, bf16[32,128,128]{2,1,0:T(8,128)(2,1)}, u32[]{:S(2)}) %copy-start.1) | copy-done | bytes 1048600
  18.9 3.8 %pack_messages.1 = bf16[16,528,128]{2,1,0:T(8,128)(2,1)S(1)} custom-call(s32[16]{0:T(128)S(1)} %slice_reduce_fusion.asked, f32[32,1,128]{2,1,0:T(1,128)S(1)} %get-tuple-element.19.rows, bf16[32,512,128]{2,1,0:T(8,128)(2,1)} %blocks.1, bf16[32,512,128]{2,1,0:T(8,128)(2,1)} %blocks.1, bf16[32,512,128]{2,1,0:T(8,128)(2,1)} %blocks.1, ...), custom_call_target="tpu_custom_call" | custom-call | tf_op jit(solution)/shard_map/pack_messages/pallas_call | solution.py:150
  22.7 0.0 copy-start.3
  22.7 1.4 %copy-done.3 = bf16[16,528,128]{2,1,0:T(8,128)(2,1)} copy-done((bf16[16,528,128]{2,1,0:T(8,128)(2,1)}, bf16[16,528,128]{2,1,0:T(8,128)(2,1)S(1)}, u32[]{:S(2)}) %copy-start.3) | copy-done | bytes 2162712
  24.1 0.0 copy-start.2
  24.1 4.6 %all-to-all-start.1 = ((bf16[16,528,128]{2,1,0:T(8,128)(2,1)}), bf16[16,528,128]{2,1,0:T(8,128)(2,1)}, u32[]{:S(2)}, u32[]{:S(2)}) async-start(bf16[16,528,128]{2,1,0:T(8,128)(2,1)} %copy-done.3), calls=%async_computation.1 | async-start | bytes 4325376 | tf_op jit(solution)/shard_map/all_to_all | solution.py:297
  28.7 0.0 copy-done.2
  28.7 0.0 copy-start.8
  28.7 0.0 copy-start.9
  28.7 0.0 copy-start.10
  28.7 5.9 %own_rotated.1.refs_0_.refs_1_.refs_2_.refs_3_ = bf16[32,128,512]{2,1,0:T(8,128)(2,1)S(1)} custom-call(bf16[32,512,128]{2,1,0:T(8,128)(2,1)} %blocks.1, bf16[32,128,128]{2,1,0:T(8,128)(2,1)S(1)} %copy-done.2), custom_call_target="tpu_custom_call" | custom-call | tf_op jit(solution)/shard_map/own_rotated/pallas_call | solution.py:116
  34.7 0.0 copy-start
  34.7 2.0 %copy-done = bf16[32,128,512]{2,1,0:T(8,128)(2,1)} copy-done((bf16[32,128,512]{2,1,0:T(8,128)(2,1)}, bf16[32,128,512]{2,1,0:T(8,128)(2,1)S(1)}, u32[]{:S(2)}) %copy-start) | copy-done | bytes 4194328
  36.6 34.3 %all-to-all-done.1.message = bf16[16,528,128]{2,1,0:T(8,128)(2,1)} async-done(((bf16[16,528,128]{2,1,0:T(8,128)(2,1)}), bf16[16,528,128]{2,1,0:T(8,128)(2,1)}, u32[]{:S(2)}, u32[]{:S(2)}) %all-to-all-start.1) | async-done | bytes 2162720 | tf_op jit(solution)/shard_map/all_to_all | solution.py:297
  70.9 0.0 copy-done.8
  70.9 0.0 copy-done.9
  70.9 0.0 copy-done.10
  70.9 0.0 copy-start.11
  70.9 15.5 %pair_terms.1 = (bf16[64,128,128]{2,1,0:T(8,128)(2,1)S(1)}, f32[64,1,128]{2,1,0:T(1,128)S(1)}, bf16[16,128,128]{2,1,0:T(8,128)(2,1)}) custom-call(s32[64]{0:T(128)S(1)} %copy-done.8, s32[64]{0:T(128)S(1)} %copy-done.9, f32[64]{0:T(128)S(1)} %copy-done.10, bf16[16,528,128]{2,1,0:T(8,128)(2,1)} %all-to-all-done.1.message, bf16[32,128,512]{2,1,0:T(8,128)(2,1)} %copy-done, ...), custom_call_target="tpu_custom_call" | custom-call | tf_op jit(solution)/shard_map/pair_terms/pallas_call | solution.py:208
  86.4 0.0 copy-start.4
  86.4 1.3 %copy-done.4 = bf16[64,128,128]{2,1,0:T(8,128)(2,1)} copy-done((bf16[64,128,128]{2,1,0:T(8,128)(2,1)}, bf16[64,128,128]{2,1,0:T(8,128)(2,1)S(1)}, u32[]{:S(2)}) %copy-start.4) | copy-done | bytes 2097176
  87.7 11.4 %all-to-all-start.2 = ((bf16[16,128,128]{2,1,0:T(8,128)(2,1)}), bf16[16,128,128]{2,1,0:T(8,128)(2,1)}, u32[]{:S(2)}, u32[]{:S(2)}) async-start(bf16[16,128,128]{2,1,0:T(8,128)(2,1)} %get-tuple-element.25), calls=%async_computation.2 | async-start | bytes 1048576 | tf_op jit(solution)/shard_map/all_to_all | solution.py:297
  99.1 0.0 copy-done.11
  99.1 0.0 copy-start.5
  99.1 1.6 %copy-done.5 = bf16[64,128,128]{2,1,0:T(8,128)(2,1)S(1)} copy-done((bf16[64,128,128]{2,1,0:T(8,128)(2,1)S(1)}, bf16[64,128,128]{2,1,0:T(8,128)(2,1)}, u32[]{:S(2)}) %copy-start.5) | copy-done | bytes 2097176
  100.7 4.3 %left_sums.1 = (f32[32,128,128]{2,1,0:T(8,128)S(1)}, f32[64,1]{1,0:T(8,128)S(1)}) custom-call(s32[64]{0:T(128)S(1)} %copy-done.11, s32[64]{0:T(128)S(1)} %copy-done.8, bf16[64,128,128]{2,1,0:T(8,128)(2,1)S(1)} %copy-done.5, f32[64,1,128]{2,1,0:T(1,128)S(1)} %get-tuple-element.22.energy), custom_call_target="tpu_custom_call" | custom-call | tf_op jit(solution)/shard_map/left_sums/pallas_call | solution.py:251
  105.0 0.6 reduce.1
  105.6 8.0 %all-to-all-done.2.right = bf16[16,128,128]{2,1,0:T(8,128)(2,1)} async-done(((bf16[16,128,128]{2,1,0:T(8,128)(2,1)}), bf16[16,128,128]{2,1,0:T(8,128)(2,1)}, u32[]{:S(2)}, u32[]{:S(2)}) %all-to-all-start.2) | async-done | bytes 524320 | tf_op jit(solution)/shard_map/all_to_all | solution.py:297
  113.6 7.3 %final_density.1 = f32[32,128,128]{2,1,0:T(8,128)} custom-call(s32[16]{0:T(128)S(1)} %slice_reduce_fusion.asked, f32[32,128,128]{2,1,0:T(8,128)S(1)} %get-tuple-element.24.inner, bf16[16,128,128]{2,1,0:T(8,128)(2,1)} %all-to-all-done.2.right, bf16[32,128,128]{2,1,0:T(8,128)(2,1)S(1)} %copy-done.2), custom_call_target="tpu_custom_call" | custom-call | tf_op jit(solution)/shard_map/final_density/pallas_call | solution.py:286
Async XLA Ops:
  3.6 13.7 %all-to-all-start = ((s32[16,1,128]{2,1,0:T(1,128)}), s32[16,1,128]{2,1,0:T(1,128)S(1)}, u32[]{:S(2)}, u32[]{:S(2)}) async-start(s32[16,1,128]{2,1,0:T(1,128)} %get-tuple-element.18), calls=%async_computation | async-start | bytes 16384 | tf_op jit(solution)/shard_map/all_to_all | solution.py:297
  11.0 0.7 copy-start.6
  11.7 0.7 copy-start.7
  17.7 1.2 %copy-start.1 = (bf16[32,128,128]{2,1,0:T(8,128)(2,1)S(1)}, bf16[32,128,128]{2,1,0:T(8,128)(2,1)}, u32[]{:S(2)}) copy-start(bf16[32,128,128]{2,1,0:T(8,128)(2,1)} %transforms.3) | copy-start | bytes 3145732
  22.7 1.4 %copy-start.3 = (bf16[16,528,128]{2,1,0:T(8,128)(2,1)}, bf16[16,528,128]{2,1,0:T(8,128)(2,1)S(1)}, u32[]{:S(2)}) copy-start(bf16[16,528,128]{2,1,0:T(8,128)(2,1)S(1)} %pack_messages.1) | copy-start | bytes 6488068
  24.1 4.6 %copy-start.2 = (bf16[32,128,128]{2,1,0:T(8,128)(2,1)S(1)}, bf16[32,128,128]{2,1,0:T(8,128)(2,1)}, u32[]{:S(2)}) copy-start(bf16[32,128,128]{2,1,0:T(8,128)(2,1)} %transforms.3) | copy-start | bytes 3145732
  24.1 46.8 %all-to-all-start.1 = ((bf16[16,528,128]{2,1,0:T(8,128)(2,1)}), bf16[16,528,128]{2,1,0:T(8,128)(2,1)}, u32[]{:S(2)}, u32[]{:S(2)}) async-start(bf16[16,528,128]{2,1,0:T(8,128)(2,1)} %copy-done.3), calls=%async_computation.1 | async-start | bytes 4325376 | tf_op jit(solution)/shard_map/all_to_all | solution.py:297
  28.7 42.2 %copy-start.8 = (s32[64]{0:T(128)S(1)}, s32[64]{0:T(128)}, u32[]{:S(2)}) copy-start(s32[64]{0:T(128)} %get-tuple-element.15.first) | copy-start | bytes 772
  28.7 42.2 %copy-start.9 = (s32[64]{0:T(128)S(1)}, s32[64]{0:T(128)}, u32[]{:S(2)}) copy-start(s32[64]{0:T(128)} %get-tuple-element.16.shift) | copy-start | bytes 772
  28.7 42.2 %copy-start.10 = (f32[64]{0:T(128)S(1)}, f32[64]{0:T(128)}, u32[]{:S(2)}) copy-start(f32[64]{0:T(128)} %get-tuple-element.17.occupied) | copy-start | bytes 772
  34.7 2.0 %copy-start = (bf16[32,128,512]{2,1,0:T(8,128)(2,1)}, bf16[32,128,512]{2,1,0:T(8,128)(2,1)S(1)}, u32[]{:S(2)}) copy-start(bf16[32,128,512]{2,1,0:T(8,128)(2,1)S(1)} %own_rotated.1.refs_0_.refs_1_.refs_2_.refs_3_) | copy-start | bytes 12582916
  70.9 28.2 %copy-start.11 = (s32[64]{0:T(128)S(1)}, s32[64]{0:T(128)}, u32[]{:S(2)}) copy-start(s32[64]{0:T(128)} %get-tuple-element.14.index) | copy-start | bytes 772
  86.4 1.3 %copy-start.4 = (bf16[64,128,128]{2,1,0:T(8,128)(2,1)}, bf16[64,128,128]{2,1,0:T(8,128)(2,1)S(1)}, u32[]{:S(2)}) copy-start(bf16[64,128,128]{2,1,0:T(8,128)(2,1)S(1)} %get-tuple-element.21.half) | copy-start | bytes 6291460
  87.7 25.9 %all-to-all-start.2 = ((bf16[16,128,128]{2,1,0:T(8,128)(2,1)}), bf16[16,128,128]{2,1,0:T(8,128)(2,1)}, u32[]{:S(2)}, u32[]{:S(2)}) async-start(bf16[16,128,128]{2,1,0:T(8,128)(2,1)} %get-tuple-element.25), calls=%async_computation.2 | async-start | bytes 1048576 | tf_op jit(solution)/shard_map/all_to_all | solution.py:297
  99.1 1.6 %copy-start.5 = (bf16[64,128,128]{2,1,0:T(8,128)(2,1)S(1)}, bf16[64,128,128]{2,1,0:T(8,128)(2,1)}, u32[]{:S(2)}) copy-start(bf16[64,128,128]{2,1,0:T(8,128)(2,1)} %copy-done.4) | copy-start | bytes 6291460

commit v2 on v0

v2 whole, which is shorter than its diff:
```python
import functools

import jax
import jax.numpy as jnp
from jax import lax
from jax.experimental import pallas as pl
from jax.experimental.pallas import tpu as pltpu
from jax.sharding import PartitionSpec as P

AUXBLK = 128
ENERGY_ROWS = 16
DIAGONAL_ROWS = 16
MIB = 1024 * 1024

SMEM = functools.partial(pl.BlockSpec, memory_space=pltpu.SMEM)
VMEM = functools.partial(pl.BlockSpec, memory_space=pltpu.VMEM)
ANY = functools.partial(pl.BlockSpec, memory_space=pl.ANY)


def in_hbm(array):
    return pltpu.with_memory_space_constraint(array, pltpu.HBM)


def f32_dot(lhs, rhs, dims):
    return lax.dot_general(lhs, rhs, (dims, ((), ())), preferred_element_type=jnp.float32)


def in_two_parts(value):
    high = value.astype(jnp.bfloat16)
    return high, (value - high.astype(jnp.float32)).astype(jnp.bfloat16)


def turned(turn, inner):
    width = inner.shape[1]
    both = f32_dot(turn, jnp.concatenate(in_two_parts(inner), axis=1), ((1,), (0,)))
    return both[:, :width] + both[:, width:]


def turned_back(half_way, turn):
    height = half_way.shape[0]
    both = f32_dot(jnp.concatenate(in_two_parts(half_way), axis=0), turn, ((1,), (1,)))
    return both[:height] + both[height:]


def plan_kernel(orb_dev, cap, pairs, slots, offsets, eps_occ, wanted, index, first, shift, occupied, seen):
    owners = wanted.shape[0]

    def clear(owner, carry):
        seen[owner] = 0
        return carry

    lax.fori_loop(0, owners, clear, 0, unroll=8)

    def one_pair(pair, carry):
        slot_i = slots[pairs[0, pair]]
        slot_j = slots[pairs[1, pair]]
        owner = lax.div(slot_j, jnp.int32(orb_dev))
        local_j = lax.rem(slot_j, jnp.int32(orb_dev))
        rank = seen[owner]
        seen[owner] = rank + 1
        place = owner * cap + rank
        index[place] = pair
        first[place] = lax.rem(slot_i, jnp.int32(orb_dev))
        shift[place] = offsets[slot_i] - offsets[slot_j]
        occupied[place] = eps_occ[slot_i] + eps_occ[slot_j]
        wanted[owner] = jnp.full(wanted.shape[1:], local_j, jnp.int32)
        return carry

    lax.fori_loop(0, pairs.shape[1], one_pair, 0, unroll=8)


def plan(owners, orb_dev, pair_list, orbital_slot, offsets, eps_occ):
    pair_dev = pair_list.shape[0]
    cap = pair_dev // owners
    sorted_ints = pltpu.HBM((pair_dev,), jnp.int32)
    return pl.pallas_call(
        functools.partial(plan_kernel, orb_dev, cap),
        out_shape=(
            pltpu.HBM((owners, 1, 128), jnp.int32),
            sorted_ints,
            sorted_ints,
            sorted_ints,
            pltpu.HBM((pair_dev,), jnp.float32),
        ),
        in_specs=[SMEM()] * 4,
        out_specs=(VMEM(), SMEM(), SMEM(), SMEM(), SMEM()),
        scratch_shapes=[pltpu.SMEM((owners,), jnp.int32)],
        name="plan",
    )(*map(in_hbm, (pair_list.T, orbital_slot, offsets, eps_occ)))


def energies_kernel(domain, eps_virt, rows):
    orb_dev, width = domain.shape
    wanted = domain[...]
    line, lane = wanted // 128, wanted % 128
    found = jnp.zeros((orb_dev, width), jnp.float32)
    for k in range(eps_virt.shape[0]):
        spread = jnp.broadcast_to(eps_virt[pl.ds(k, 1), :], (orb_dev, width))
        picked = jnp.take_along_axis(spread, lane, axis=1)
        found = jnp.where(line == k, picked, found)
    found = found.astype(jnp.bfloat16).astype(jnp.float32)
    for s in range(orb_dev):
        rows[s] = found[s : s + 1, :]


def domain_energies(domain, eps_virt):
    orb_dev, width = domain.shape
    return pl.pallas_call(
        energies_kernel,
        in_specs=[VMEM()] * 2,
        out_specs=VMEM(),
        out_shape=pltpu.HBM((orb_dev, 1, width), jnp.float32),
        name="domain_energies",
    )(*map(in_hbm, (domain, eps_virt.reshape(-1, 128))))


def own_kernel(chunk, blocks, transforms, held, block_rows, turns, made, arrived, left):
    chunks = blocks.shape[0] // chunk

    def coming(c):
        part = pl.ds(c * chunk, chunk)
        return (
            pltpu.make_async_copy(blocks.at[part], block_rows.at[part], arrived.at[0, c]),
            pltpu.make_async_copy(transforms.at[part], turns.at[part], arrived.at[1, c]),
        )

    def going(c):
        part = pl.ds(c * chunk, chunk)
        return pltpu.make_async_copy(made.at[part], held.at[part], left.at[c])

    for c in range(chunks):
        for copy in coming(c):
            copy.start()

    def one_chunk(c, carry):
        for copy in coming(c):
            copy.wait()
        slots = [c * chunk + u for u in range(chunk)]
        rotated = [f32_dot(block_rows[slot], turns[slot], ((1,), (0,))) for slot in slots]
        for slot, one in zip(slots, rotated):
            made[slot] = one.astype(jnp.bfloat16)
        going(c).start()
        return carry

    lax.fori_loop(0, chunks, one_chunk, 0)
    for c in range(chunks):
        going(c).wait()


def own_rotated(blocks, transforms, chunk=4):
    orb_dev = blocks.shape[0]
    return pl.pallas_call(
        functools.partial(own_kernel, chunk),
        in_specs=[ANY()] * 2,
        out_specs=ANY(),
        out_shape=pltpu.HBM(blocks.shape, jnp.bfloat16),
        scratch_shapes=[
            pltpu.VMEM(blocks.shape, jnp.bfloat16),
            pltpu.VMEM(transforms.shape, jnp.bfloat16),
            pltpu.VMEM(blocks.shape, jnp.bfloat16),
            pltpu.SemaphoreType.DMA((2, orb_dev // chunk)),
            pltpu.SemaphoreType.DMA((orb_dev // chunk,)),
        ],
        compiler_params=pltpu.CompilerParams(vmem_limit_bytes=16 * MIB),
        name="own_rotated",
    )(*map(in_hbm, (blocks, transforms)))


def pack_kernel(
    batch, asked, rows, blocks, transforms, messages, block_rows, turns, made, arrived, left
):
    owners = messages.shape[0]
    fit_rows, width = blocks.shape[1:]

    def coming(owner):
        slot = asked[owner, 0, 0]
        return (
            pltpu.make_async_copy(blocks.at[slot], block_rows.at[owner], arrived.at[0, owner]),
            pltpu.make_async_copy(transforms.at[slot], turns.at[owner], arrived.at[1, owner]),
        )

    def going(owner):
        return pltpu.make_async_copy(made.at[owner], messages.at[owner], left.at[owner])

    def start(owner, carry):
        for copy in coming(owner):
            copy.start()
        return carry

    def forward(b, carry):
        group = [b * batch + u for u in range(batch)]
        for owner in group:
            for copy in coming(owner):
                copy.wait()
        rotated = [f32_dot(block_rows[owner], turns[owner], ((1,), (0,))) for owner in group]
        for owner, one in zip(group, rotated):
            made[owner, :fit_rows, :] = one.astype(jnp.bfloat16)
            energy = rows[asked[owner, 0, 0]]
            made[owner, fit_rows:, :] = jnp.broadcast_to(energy, (ENERGY_ROWS, width)).astype(
                jnp.bfloat16
            )
        for owner in group:
            going(owner).start()
        return carry

    def finish(owner, carry):
        going(owner).wait()
        return carry

    lax.fori_loop(0, owners, start, 0)
    lax.fori_loop(0, owners // batch, forward, 0)
    lax.fori_loop(0, owners, finish, 0)


def pack_messages(asked, rows, blocks, transforms, batch=4):
    owners = asked.shape[0]
    _, fit_rows, width = blocks.shape
    shape = (owners, fit_rows + ENERGY_ROWS, width)
    return pl.pallas_call(
        functools.partial(pack_kernel, batch),
        in_specs=[SMEM(), VMEM(), ANY(), ANY()],
        out_specs=ANY(),
        out_shape=pltpu.HBM(shape, jnp.bfloat16),
        scratch_shapes=[
            pltpu.VMEM((owners, fit_rows, width), jnp.bfloat16),
            pltpu.VMEM((owners, width, width), jnp.bfloat16),
            pltpu.VMEM(shape, jnp.bfloat16),
            pltpu.SemaphoreType.DMA((2, owners)),
            pltpu.SemaphoreType.DMA((owners,)),
        ],
        compiler_params=pltpu.CompilerParams(vmem_limit_bytes=(2 + owners // 2) * MIB),
        name="pack_messages",
    )(asked, *map(in_hbm, (rows, blocks, transforms)))


def fold_symmetric(full):
    width = full.shape[0]
    mid = width // 2
    row = lax.broadcasted_iota(jnp.int32, (mid, width), 0)
    lane = lax.broadcasted_iota(jnp.int32, (mid, width), 1)
    upper, lower = full[:mid, :], full[mid:, :]
    folded = jnp.where(lane <= row + mid, pltpu.roll(upper, mid, 1), lower)
    diagonal = jnp.sum(jnp.where(lane == row + mid, lower, 0.0), axis=0, keepdims=True)
    return jnp.concatenate([folded, jnp.broadcast_to(diagonal, (DIAGONAL_ROWS, width))], axis=0)


def unfold_symmetric(folded):
    width = folded.shape[1]
    mid = width // 2
    row = lax.broadcasted_iota(jnp.int32, (mid, width), 0)
    lane = lax.broadcasted_iota(jnp.int32, (mid, width), 1)
    body, diagonal = folded[:mid, :], folded[mid : mid + 1, :]
    moved = pltpu.roll(body, mid, 1)
    upper = jnp.where(lane < row, moved, 0.0) + jnp.where(lane >= mid, moved, 0.0)
    upper = upper + jnp.where(lane == row, 0.5 * moved, 0.0)
    lower = jnp.where(lane > row + mid, body, 0.0)
    lower = lower + jnp.where(lane == row + mid, 0.5 * diagonal, 0.0)
    once = jnp.concatenate([upper, lower], axis=0)
    return once + once.T


def pairs_kernel(
    cap, batch, first, shift, occupied, rows, held, came, half, energy, right, made, left
):
    steps, height, width = came.shape
    fit_rows = height - ENERGY_ROWS
    block_count = fit_rows // AUXBLK

    def going(b):
        part = pl.ds(b * batch * cap, batch * cap)
        return pltpu.make_async_copy(made.at[part], half.at[part], left.at[b])

    def shifted(place):
        moved = []
        for block in range(block_count):
            source = block - shift[place]
            inside = (source >= 0) & (source < block_count)
            begin = pl.multiple_of(jnp.clip(source, 0, block_count - 1) * AUXBLK, AUXBLK)
            part = held[first[place], pl.ds(begin, AUXBLK), :]
            moved.append(jnp.where(inside, part, jnp.zeros_like(part)))
        return jnp.concatenate(moved, axis=0)

    def one_batch(b, carry):
        group = [b * batch + u for u in range(batch)]
        couplings, far = [], []
        for step in group:
            side = jnp.concatenate([shifted(step * cap + k) for k in range(cap)], axis=1)
            couplings.append(f32_dot(came[step, :fit_rows, :].T, side, ((1,), (0,))))
            row = came[step, fit_rows:, :].astype(jnp.float32)[:1, :]
            far.append(jnp.broadcast_to(row, (width, width)).T)
        for u, step in enumerate(group):
            halves = []
            for k in range(cap):
                place = step * cap + k
                coupling = couplings[u][:, k * width : (k + 1) * width]
                amplitude = coupling / (far[u] + (rows[first[place]] - occupied[place]))
                energy[place] = jnp.sum(coupling * amplitude, axis=0, keepdims=True)
                halves.append(amplitude.astype(jnp.bfloat16))
                made[place] = halves[-1]
            side = jnp.concatenate(halves, axis=1)
            density = f32_dot(side, side, ((1,), (1,)))
            right[step] = fold_symmetric(density).astype(jnp.bfloat16)
        going(b).start()
        return carry

    def finish(b, carry):
        going(b).wait()
        return carry

    lax.fori_loop(0, steps // batch, one_batch, 0)
    lax.fori_loop(0, steps // batch, finish, 0)


def pair_terms(first, shift, occupied, rows, held, messages, batch=8):
    steps, height, width = messages.shape
    pair_dev = first.shape[0]
    cap = pair_dev // steps
    return pl.pallas_call(
        functools.partial(pairs_kernel, cap, batch),
        in_specs=[SMEM()] * 3 + [VMEM()] * 3,
        out_specs=(ANY(), VMEM(), VMEM()),
        out_shape=(
            pltpu.HBM((pair_dev, width, width), jnp.bfloat16),
            pltpu.HBM((pair_dev, 1, width), jnp.float32),
            pltpu.HBM((steps, width // 2 + DIAGONAL_ROWS, width), jnp.bfloat16),
        ),
        scratch_shapes=[
            pltpu.VMEM((pair_dev, width, width), jnp.bfloat16),
            pltpu.SemaphoreType.DMA((steps // batch,)),
        ],
        compiler_params=pltpu.CompilerParams(vmem_limit_bytes=24 * MIB),
        name="pair_terms",
    )(*map(in_hbm, (first, shift, occupied, rows)), held, messages)


def left_kernel(
    batch, index, first, half, energy, transforms, density, pair_energy, halves, turns, inner, scattered, arrived
):
    orb_dev, width, _ = inner.shape
    pair_dev = half.shape[0]
    loads = [
        pltpu.make_async_copy(half, halves, arrived.at[0]),
        pltpu.make_async_copy(transforms, turns, arrived.at[1]),
    ]
    for load in loads:
        load.start()
    inner[...] = jnp.zeros_like(inner)
    for load in loads:
        load.wait()

    def some_pairs(b, carry):
        places = [b * batch + u for u in range(batch)]
        sums = [f32_dot(halves[place], halves[place], ((0,), (0,))) for place in places]
        for place, one in zip(places, sums):
            slot = first[place]
            inner[slot] = inner[slot] + one
            scattered[index[place]] = energy[place]
        return carry

    lax.fori_loop(0, pair_dev // batch, some_pairs, 0)

    def some_slots(b, carry):
        slots = [b * batch + u for u in range(batch)]
        half_way = [turned(turns[slot], inner[slot]) for slot in slots]
        for slot, one in zip(slots, half_way):
            density[slot] = turned_back(one, turns[slot])
        return carry

    lax.fori_loop(0, orb_dev // batch, some_slots, 0)
    gathered = scattered[...].reshape(pair_dev, width)
    pair_energy[...] = -jnp.sum(gathered.T, axis=0, keepdims=True) / width


def left_density(index, first, half, energy, transforms, batch=8):
    orb_dev = transforms.shape[0]
    pair_dev, width, _ = half.shape
    return pl.pallas_call(
        functools.partial(left_kernel, batch),
        in_specs=[SMEM(), SMEM(), ANY(), VMEM(), ANY()],
        out_specs=(VMEM(), VMEM()),
        out_shape=(
            pltpu.HBM((orb_dev, width, width), jnp.float32),
            pltpu.HBM((1, pair_dev), jnp.float32),
        ),
        scratch_shapes=[
            pltpu.VMEM(half.shape, jnp.bfloat16),
            pltpu.VMEM(transforms.shape, jnp.bfloat16),
            pltpu.VMEM((orb_dev, width, width), jnp.float32),
            pltpu.VMEM((pair_dev, 1, width), jnp.float32),
            pltpu.SemaphoreType.DMA((2,)),
        ],
        compiler_params=pltpu.CompilerParams(vmem_limit_bytes=16 * MIB),
        name="left_density",
    )(*map(in_hbm, (index, first, half, energy, transforms)))


def right_kernel(
    batch, asked, density, rights, transforms, out, total, turns, arrived, left
):
    loads = [
        pltpu.make_async_copy(transforms, turns, arrived.at[0]),
        pltpu.make_async_copy(density, total, arrived.at[1]),
    ]
    for load in loads:
        load.start()
    for load in loads:
        load.wait()

    def some_messages(b, carry):
        slots = [asked[b * batch + u, 0, 0] for u in range(batch)]
        inner = [
            unfold_symmetric(rights[b * batch + u].astype(jnp.float32)).astype(jnp.bfloat16)
            for u in range(batch)
        ]
        half_way = [f32_dot(turns[slot], one, ((1,), (0,))) for slot, one in zip(slots, inner)]
        parts = [turned_back(one, turns[slot]) for slot, one in zip(slots, half_way)]
        for slot, part in zip(slots, parts):
            total[slot] = total[slot] + part
        return carry

    lax.fori_loop(0, rights.shape[0] // batch, some_messages, 0)
    store = pltpu.make_async_copy(total, out, left.at[0])
    store.start()
    store.wait()


def add_right_density(asked, density, right, transforms, batch=8):
    return pl.pallas_call(
        functools.partial(right_kernel, batch),
        in_specs=[SMEM(), ANY(), VMEM(), ANY()],
        out_specs=ANY(),
        out_shape=pltpu.HBM(density.shape, jnp.float32),
        scratch_shapes=[
            pltpu.VMEM(density.shape, jnp.float32),
            pltpu.VMEM(transforms.shape, jnp.bfloat16),
            pltpu.SemaphoreType.DMA((2,)),
            pltpu.SemaphoreType.DMA((1,)),
        ],
        compiler_params=pltpu.CompilerParams(vmem_limit_bytes=16 * MIB),
        name="add_right_density",
    )(asked, in_hbm(density), right, in_hbm(transforms))


def exchange(messages):
    return lax.all_to_all(messages, "orb", split_axis=0, concat_axis=0, tiled=True)


def local(pair_list, orbital_slot, blocks, transforms, domain, eps_virt, eps_occ, offsets):
    owners = lax.axis_size("orb")
    orb_dev = blocks.shape[0]
    wanted, index, first, shift, occupied = plan(
        owners, orb_dev, pair_list, orbital_slot, offsets, eps_occ
    )
    asked = exchange(wanted)
    rows = domain_energies(domain, eps_virt)
    incoming = exchange(pack_messages(asked, rows, blocks, transforms))
    held = own_rotated(blocks, transforms)
    half, energy, right = pair_terms(first, shift, occupied, rows, held, incoming)
    came_back = exchange(right)
    density, pair_energy = left_density(index, first, half, energy, transforms)
    density = add_right_density(asked, density, came_back, transforms)
    return (pair_energy.reshape(-1), density)


def solution(mesh):
    in_specs = (
        P(("groups", "orb"), None),
        P("groups"),
        P(("groups", "orb"), None, None),
        P(("groups", "orb"), None, None),
        P(("groups", "orb"), None),
        P("groups"),
        P("groups"),
        P("groups"),
    )
    out_specs = (P(("groups", "orb")), P(("groups", "orb"), None, None))
    return jax.shard_map(local, mesh=mesh, in_specs=in_specs, out_specs=out_specs, check_vma=False)
```

time: 403 us -> 103 us (0.26)
  the two profiles are of different devices: /device:TPU:13 before, /device:TPU:0 now
where the time goes in v2:
time: 103 us
  waiting for transfers between devices  45.9 us (45%)
  Pallas kernels  31.4 us (30%)
  starting transfers between devices  22.6 us (22%)
  local copies, waits for them, and re-layouts  2.19 us (2%)
    all_to_all x3, waiting for transfers between devices, exchange(): lax.all_to_all(messages, 'orb', split_axis=0, concat_axis=0, tiled=True)  45.9 us
    all_to_all x3, starting transfers between devices, exchange(): lax.all_to_all(messages, 'orb', split_axis=0, concat_axis=0, tiled=True)  22.6 us
    pallas_call x1, Pallas kernels, left_density(): pl.pallas_call(functools.partial(left_kernel, batch), in_specs=[SMEM(), S...  7.89 us
    pallas_call x1, Pallas kernels, pair_terms(): pl.pallas_call(functools.partial(pairs_kernel, cap, batch), in_specs=[SME...  5.81 us
    pallas_call x1, Pallas kernels, add_right_density(): pl.pallas_call(functools.partial(right_kernel, batch), in_specs=[SMEM(),...  5.22 us
    pallas_call x1, Pallas kernels, pack_messages(): pl.pallas_call(functools.partial(pack_kernel, batch), in_specs=[SMEM(), V...  4.37 us
    pallas_call x1, Pallas kernels, own_rotated(): pl.pallas_call(functools.partial(own_kernel, chunk), in_specs=[ANY()] * 2...  4.36 us
    pallas_call x1, Pallas kernels, plan(): pl.pallas_call(functools.partial(plan_kernel, orb_dev, cap), out_shape=(p...  2.23 us
  transfers between devices with their start and end apart: 3, of which 3 were waited for; matrix products, arithmetic and copies ran while one was open for 0% of the time, Pallas kernels for 13%

profile of v2, /device:TPU:0, one launch (start us, length us, event | category | flops | bytes accessed | tf_op | source)
XLA Modules:
  0.0 102.7 jit_solution(1264742379392875662)
XLA Ops:
  0.6 2.2 %plan.1 = (s32[16,1,128]{2,1,0:T(1,128)}, s32[64]{0:T(128)}, s32[64]{0:T(128)}, s32[64]{0:T(128)}, f32[64]{0:T(128)}) custom-call(s32[2,64]{1,0:T(2,128)} %bitcast.4, s32[512]{0:T(512)} %slots.1, s32[512]{0:T(512)} %offsets.1, f32[512]{0:T(512)} %eps_occ.1), custom_call_target="tpu_custom_call" | custom-call | tf_op jit(solution)/shard_map/plan/pallas_call | solution.py:76
  2.9 7.4 %all-to-all-start = ((s32[16,1,128]{2,1,0:T(1,128)}), s32[16,1,128]{2,1,0:T(1,128)S(1)}, u32[]{:S(2)}, u32[]{:S(2)}) async-start(s32[16,1,128]{2,1,0:T(1,128)} %get-tuple-element.16), calls=%async_computation | async-start | bytes 16384 | tf_op jit(solution)/shard_map/all_to_all | solution.py:445
  10.3 1.5 %domain_energies.1.rows = f32[32,1,128]{2,1,0:T(1,128)} custom-call(s32[32,128]{1,0:T(8,128)} %domain.1, f32[16,128]{1,0:T(8,128)} %bitcast.3), custom_call_target="tpu_custom_call" | custom-call | tf_op jit(solution)/shard_map/domain_energies/pallas_call | solution.py:108
  11.8 4.8 %all-to-all-done.asked = s32[16,1,128]{2,1,0:T(1,128)S(1)} async-done(((s32[16,1,128]{2,1,0:T(1,128)}), s32[16,1,128]{2,1,0:T(1,128)S(1)}, u32[]{:S(2)}, u32[]{:S(2)}) %all-to-all-start) | async-done | bytes 8224 | tf_op jit(solution)/shard_map/all_to_all | solution.py:445
  16.6 4.4 %pack_messages.1 = bf16[16,528,128]{2,1,0:T(8,128)(2,1)} custom-call(s32[16,1,128]{2,1,0:T(1,128)S(1)} %all-to-all-done.asked, f32[32,1,128]{2,1,0:T(1,128)} %domain_energies.1.rows, bf16[32,512,128]{2,1,0:T(8,128)(2,1)} %blocks.3, bf16[32,128,128]{2,1,0:T(8,128)(2,1)} %transforms.7), custom_call_target="tpu_custom_call" | custom-call | tf_op jit(solution)/shard_map/pack_messages/pallas_call | solution.py:219
  21.0 3.7 %all-to-all-start.1 = ((bf16[16,528,128]{2,1,0:T(8,128)(2,1)}), bf16[16,528,128]{2,1,0:T(8,128)(2,1)S(1)}, u32[]{:S(2)}, u32[]{:S(2)}) async-start(bf16[16,528,128]{2,1,0:T(8,128)(2,1)} %pack_messages.1), calls=%async_computation.1 | async-start | bytes 4325376 | tf_op jit(solution)/shard_map/all_to_all | solution.py:445
  24.7 4.4 %own_rotated.1.held = bf16[32,512,128]{2,1,0:T(8,128)(2,1)} custom-call(bf16[32,512,128]{2,1,0:T(8,128)(2,1)} %blocks.3, bf16[32,128,128]{2,1,0:T(8,128)(2,1)} %transforms.7), custom_call_target="tpu_custom_call" | custom-call | tf_op jit(solution)/shard_map/own_rotated/pallas_call | solution.py:152
  29.1 37.8 %all-to-all-done.1.came = bf16[16,528,128]{2,1,0:T(8,128)(2,1)S(1)} async-done(((bf16[16,528,128]{2,1,0:T(8,128)(2,1)}), bf16[16,528,128]{2,1,0:T(8,128)(2,1)S(1)}, u32[]{:S(2)}, u32[]{:S(2)}) %all-to-all-start.1) | async-done | bytes 2162720 | tf_op jit(solution)/shard_map/all_to_all | solution.py:445
  66.9 0.0 copy-start
  66.9 2.2 %copy-done = bf16[32,512,128]{2,1,0:T(8,128)(2,1)S(1)} copy-done((bf16[32,512,128]{2,1,0:T(8,128)(2,1)S(1)}, bf16[32,512,128]{2,1,0:T(8,128)(2,1)}, u32[]{:S(2)}) %copy-start) | copy-done | bytes 4194328
  69.1 5.8 %pair_terms.1 = (bf16[64,128,128]{2,1,0:T(8,128)(2,1)}, f32[64,1,128]{2,1,0:T(1,128)}, bf16[16,80,128]{2,1,0:T(8,128)(2,1)}) custom-call(s32[64]{0:T(128)} %get-tuple-element.13.first, s32[64]{0:T(128)} %get-tuple-element.14.shift, f32[64]{0:T(128)} %get-tuple-element.15.occupied, f32[32,1,128]{2,1,0:T(1,128)} %domain_energies.1.rows, ...), custom_call_target="tpu_custom_call" | custom-call | tf_op jit(solution)/shard_map/pair_terms/pallas_call | solution.py:318
  74.9 11.5 %all-to-all-start.2 = ((bf16[16,80,128]{2,1,0:T(8,128)(2,1)}), bf16[16,80,128]{2,1,0:T(8,128)(2,1)S(1)}, u32[]{:S(2)}, u32[]{:S(2)}) async-start(bf16[16,80,128]{2,1,0:T(8,128)(2,1)} %get-tuple-element.21), calls=%async_computation.2 | async-start | bytes 655360 | tf_op jit(solution)/shard_map/all_to_all | solution.py:445
  86.4 7.9 %left_density.1 = (f32[32,128,128]{2,1,0:T(8,128)}, f32[1,64]{1,0:T(1,128)}) custom-call(s32[64]{0:T(128)} %get-tuple-element.12.index, s32[64]{0:T(128)} %get-tuple-element.13.first, bf16[64,128,128]{2,1,0:T(8,128)(2,1)} %get-tuple-element.17.half, f32[64,1,128]{2,1,0:T(1,128)} %get-tuple-element.18.energy, bf16[32,128,128]{2,1,0:T(8,128)(2,1)} %transforms.7), custom_call_target="tpu_custom_call" | custom-call | tf_op jit(solution)/shard_map/left_density/pallas_call | solution.py:377
  94.3 3.2 %all-to-all-done.2.rights = bf16[16,80,128]{2,1,0:T(8,128)(2,1)S(1)} async-done(((bf16[16,80,128]{2,1,0:T(8,128)(2,1)}), bf16[16,80,128]{2,1,0:T(8,128)(2,1)S(1)}, u32[]{:S(2)}, u32[]{:S(2)}) %all-to-all-start.2) | async-done | bytes 327712 | tf_op jit(solution)/shard_map/all_to_all | solution.py:445
  97.5 5.2 %add_right_density.1 = f32[32,128,128]{2,1,0:T(8,128)} custom-call(s32[16,1,128]{2,1,0:T(1,128)S(1)} %all-to-all-done.asked, f32[32,128,128]{2,1,0:T(8,128)} %get-tuple-element.20.density, bf16[16,80,128]{2,1,0:T(8,128)(2,1)S(1)} %all-to-all-done.2.rights, bf16[32,128,128]{2,1,0:T(8,128)(2,1)} %transforms.7), custom_call_target="tpu_custom_call" | custom-call | tf_op jit(solution)/shard_map/add_right_density/pallas_call | solution.py:428
Async XLA Ops:
  2.9 13.7 %all-to-all-start = ((s32[16,1,128]{2,1,0:T(1,128)}), s32[16,1,128]{2,1,0:T(1,128)S(1)}, u32[]{:S(2)}, u32[]{:S(2)}) async-start(s32[16,1,128]{2,1,0:T(1,128)} %get-tuple-element.16), calls=%async_computation | async-start | bytes 16384 | tf_op jit(solution)/shard_map/all_to_all | solution.py:445
  21.0 45.9 %all-to-all-start.1 = ((bf16[16,528,128]{2,1,0:T(8,128)(2,1)}), bf16[16,528,128]{2,1,0:T(8,128)(2,1)S(1)}, u32[]{:S(2)}, u32[]{:S(2)}) async-start(bf16[16,528,128]{2,1,0:T(8,128)(2,1)} %pack_messages.1), calls=%async_computation.1 | async-start | bytes 4325376 | tf_op jit(solution)/shard_map/all_to_all | solution.py:445
  66.9 2.2 %copy-start = (bf16[32,512,128]{2,1,0:T(8,128)(2,1)S(1)}, bf16[32,512,128]{2,1,0:T(8,128)(2,1)}, u32[]{:S(2)}) copy-start(bf16[32,512,128]{2,1,0:T(8,128)(2,1)} %own_rotated.1.held) | copy-start | bytes 12582916
  74.9 22.6 %all-to-all-start.2 = ((bf16[16,80,128]{2,1,0:T(8,128)(2,1)}), bf16[16,80,128]{2,1,0:T(8,128)(2,1)S(1)}, u32[]{:S(2)}, u32[]{:S(2)}) async-start(bf16[16,80,128]{2,1,0:T(8,128)(2,1)} %get-tuple-element.21), calls=%async_computation.2 | async-start | bytes 655360 | tf_op jit(solution)/shard_map/all_to_all | solution.py:445

commit v3 on v2

v3 whole, which is shorter than its diff:
```python
import functools

import jax
import jax.numpy as jnp
from jax import lax
from jax.experimental import pallas as pl
from jax.experimental.pallas import tpu as pltpu
from jax.sharding import PartitionSpec as P

AUXBLK = 128
ENERGY_ROWS = 16
DIAGONAL_ROWS = 16
MIB = 1024 * 1024

SMEM = functools.partial(pl.BlockSpec, memory_space=pltpu.SMEM)
VMEM = functools.partial(pl.BlockSpec, memory_space=pltpu.VMEM)
ANY = functools.partial(pl.BlockSpec, memory_space=pl.ANY)


def in_hbm(array):
    return pltpu.with_memory_space_constraint(array, pltpu.HBM)


def f32_dot(lhs, rhs, dims):
    return lax.dot_general(lhs, rhs, (dims, ((), ())), preferred_element_type=jnp.float32)


def in_two_parts(value):
    high = value.astype(jnp.bfloat16)
    return high, (value - high.astype(jnp.float32)).astype(jnp.bfloat16)


def turned(turn, inner):
    width = inner.shape[1]
    both = f32_dot(turn, jnp.concatenate(in_two_parts(inner), axis=1), ((1,), (0,)))
    return both[:, :width] + both[:, width:]


def turned_back(half_way, turn):
    height = half_way.shape[0]
    both = f32_dot(jnp.concatenate(in_two_parts(half_way), axis=0), turn, ((1,), (1,)))
    return both[:height] + both[height:]


def wanted_kernel(orb_dev, mask, pairs, slots, wanted):
    def one_pair(pair, carry):
        slot = slots[pairs[1, pair]]
        owner = lax.div(slot, jnp.int32(orb_dev))
        local_slot = lax.rem(slot, jnp.int32(orb_dev))
        wanted[owner ^ mask] = jnp.full(wanted.shape[1:], local_slot, jnp.int32)
        return carry

    lax.fori_loop(0, pairs.shape[1], one_pair, 0, unroll=16)


def wanted_slots(owners, orb_dev, mask, pair_list, orbital_slot):
    return pl.pallas_call(
        functools.partial(wanted_kernel, orb_dev, mask),
        out_shape=pltpu.HBM((owners, 1, 128), jnp.int32),
        in_specs=[SMEM()] * 2,
        out_specs=VMEM(),
        name="wanted_slots",
    )(*map(in_hbm, (pair_list.T, orbital_slot)))


def plan_kernel(orb_dev, cap, pairs, slots, offsets, eps_occ, index, first, shift, occupied, seen):
    owners = seen.shape[0]

    def clear(owner, carry):
        seen[owner] = 0
        return carry

    lax.fori_loop(0, owners, clear, 0, unroll=8)

    def one_pair(pair, carry):
        slot_i = slots[pairs[0, pair]]
        slot_j = slots[pairs[1, pair]]
        owner = lax.div(slot_j, jnp.int32(orb_dev))
        rank = seen[owner]
        seen[owner] = rank + 1
        place = owner * cap + rank
        index[place] = pair
        first[place] = lax.rem(slot_i, jnp.int32(orb_dev))
        shift[place] = offsets[slot_i] - offsets[slot_j]
        occupied[place] = eps_occ[slot_i] + eps_occ[slot_j]
        return carry

    lax.fori_loop(0, pairs.shape[1], one_pair, 0, unroll=8)


def plan(owners, orb_dev, pair_list, orbital_slot, offsets, eps_occ):
    pair_dev = pair_list.shape[0]
    cap = pair_dev // owners
    sorted_ints = pltpu.HBM((pair_dev,), jnp.int32)
    return pl.pallas_call(
        functools.partial(plan_kernel, orb_dev, cap),
        out_shape=(
            sorted_ints,
            sorted_ints,
            sorted_ints,
            pltpu.HBM((pair_dev,), jnp.float32),
        ),
        in_specs=[SMEM()] * 4,
        out_specs=(SMEM(), SMEM(), SMEM(), SMEM()),
        scratch_shapes=[pltpu.SMEM((owners,), jnp.int32)],
        name="plan",
    )(*map(in_hbm, (pair_list.T, orbital_slot, offsets, eps_occ)))


def own_kernel(
    chunk, domain, eps_virt, blocks, transforms, rows, held, block_rows, turns, made, arrived, left
):
    orb_dev, fit_rows, width = blocks.shape
    chunks = orb_dev // chunk

    def coming(c):
        part = pl.ds(c * chunk, chunk)
        return (
            pltpu.make_async_copy(blocks.at[part], block_rows.at[part], arrived.at[0, c]),
            pltpu.make_async_copy(transforms.at[part], turns.at[part], arrived.at[1, c]),
        )

    def going(c):
        part = pl.ds(c * chunk, chunk)
        return pltpu.make_async_copy(made.at[part], held.at[part], left.at[c])

    for c in range(chunks):
        for copy in coming(c):
            copy.start()
    wanted = domain[...]
    line, lane = wanted // 128, wanted % 128
    found = jnp.zeros((orb_dev, width), jnp.float32)
    for k in range(eps_virt.shape[0]):
        spread = jnp.broadcast_to(eps_virt[pl.ds(k, 1), :], (orb_dev, width))
        picked = jnp.take_along_axis(spread, lane, axis=1)
        found = jnp.where(line == k, picked, found)
    rounded = found.astype(jnp.bfloat16).astype(jnp.float32)
    for s in range(orb_dev):
        row = rounded[s : s + 1, :]
        rows[s] = row
        made[s, fit_rows:, :] = jnp.broadcast_to(row, (ENERGY_ROWS, width)).astype(jnp.bfloat16)

    def one_chunk(c, carry):
        for copy in coming(c):
            copy.wait()
        slots = [c * chunk + u for u in range(chunk)]
        rotated = [f32_dot(block_rows[slot], turns[slot], ((1,), (0,))) for slot in slots]
        for slot, one in zip(slots, rotated):
            made[slot, :fit_rows, :] = one.astype(jnp.bfloat16)
        going(c).start()
        return carry

    lax.fori_loop(0, chunks, one_chunk, 0)
    for c in range(chunks):
        going(c).wait()


def own_rotated(domain, eps_virt, blocks, transforms, chunk=4):
    orb_dev, fit_rows, width = blocks.shape
    shape = (orb_dev, fit_rows + ENERGY_ROWS, width)
    return pl.pallas_call(
        functools.partial(own_kernel, chunk),
        in_specs=[VMEM(), VMEM(), ANY(), ANY()],
        out_specs=(VMEM(), ANY()),
        out_shape=(
            pltpu.HBM((orb_dev, 1, width), jnp.float32),
            pltpu.HBM(shape, jnp.bfloat16),
        ),
        scratch_shapes=[
            pltpu.VMEM(blocks.shape, jnp.bfloat16),
            pltpu.VMEM(transforms.shape, jnp.bfloat16),
            pltpu.VMEM(shape, jnp.bfloat16),
            pltpu.SemaphoreType.DMA((2, orb_dev // chunk)),
            pltpu.SemaphoreType.DMA((orb_dev // chunk,)),
        ],
        compiler_params=pltpu.CompilerParams(vmem_limit_bytes=16 * MIB),
        name="own_rotated",
    )(*map(in_hbm, (domain, eps_virt.reshape(-1, 128), blocks, transforms)))


def pack_kernel(asked_mask, mask, asked, held, messages, made, arrived, left):
    owners = messages.shape[0]

    def coming(owner):
        source = held.at[asked[owner ^ asked_mask, 0, 0]]
        return pltpu.make_async_copy(source, made.at[owner], arrived.at[owner])

    def going(owner):
        return pltpu.make_async_copy(made.at[owner], messages.at[owner ^ mask], left.at[owner])

    def start(owner, carry):
        coming(owner).start()
        return carry

    def forward(owner, carry):
        coming(owner).wait()
        going(owner).start()
        return carry

    def finish(owner, carry):
        going(owner).wait()
        return carry

    for step in (start, forward, finish):
        lax.fori_loop(0, owners, step, 0, unroll=4)


def pack_messages(asked_mask, mask, asked, held):
    owners = asked.shape[0]
    shape = (owners,) + held.shape[1:]
    return pl.pallas_call(
        functools.partial(pack_kernel, asked_mask, mask),
        in_specs=[SMEM(), ANY()],
        out_specs=ANY(),
        out_shape=pltpu.HBM(shape, jnp.bfloat16),
        scratch_shapes=[
            pltpu.VMEM(shape, jnp.bfloat16),
            pltpu.SemaphoreType.DMA((owners,)),
            pltpu.SemaphoreType.DMA((owners,)),
        ],
        compiler_params=pltpu.CompilerParams(vmem_limit_bytes=16 * MIB),
        name="pack_messages",
    )(asked, in_hbm(held))


def fold_symmetric(full):
    width = full.shape[0]
    mid = width // 2
    row = lax.broadcasted_iota(jnp.int32, (mid, width), 0)
    lane = lax.broadcasted_iota(jnp.int32, (mid, width), 1)
    upper, lower = full[:mid, :], full[mid:, :]
    folded = jnp.where(lane <= row + mid, pltpu.roll(upper, mid, 1), lower)
    diagonal = jnp.sum(jnp.where(lane == row + mid, lower, 0.0), axis=0, keepdims=True)
    return jnp.concatenate([folded, jnp.broadcast_to(diagonal, (DIAGONAL_ROWS, width))], axis=0)


def unfold_symmetric(folded):
    width = folded.shape[1]
    mid = width // 2
    row = lax.broadcasted_iota(jnp.int32, (mid, width), 0)
    lane = lax.broadcasted_iota(jnp.int32, (mid, width), 1)
    body, diagonal = folded[:mid, :], folded[mid : mid + 1, :]
    moved = pltpu.roll(body, mid, 1)
    upper = jnp.where(lane < row, moved, 0.0) + jnp.where(lane >= mid, moved, 0.0)
    upper = upper + jnp.where(lane == row, 0.5 * moved, 0.0)
    lower = jnp.where(lane > row + mid, body, 0.0)
    lower = lower + jnp.where(lane == row + mid, 0.5 * diagonal, 0.0)
    once = jnp.concatenate([upper, lower], axis=0)
    return once + once.T


def pairs_kernel(cap, batch, parts, mask, right_mask, *refs):
    inputs, (half, energy, right), scratch = refs[:5], refs[6:9], refs[9:]
    came = refs[5]
    first, shift, occupied, rows, held, turned_over, halves, energies, rights, arrived, left = scratch
    steps, height, width = came.shape
    fit_rows = height - ENERGY_ROWS
    block_count = fit_rows // AUXBLK
    orb_dev = rows.shape[0]
    each = orb_dev // parts

    def own(c):
        slots = pl.ds(c * each, each)
        source = inputs[4].at[slots, pl.ds(0, fit_rows)]
        return pltpu.make_async_copy(source, held.at[slots], arrived.at[4 + c])

    loads = [
        pltpu.make_async_copy(source, target, arrived.at[n])
        for n, (source, target) in enumerate(zip(inputs[:4], (first, shift, occupied, rows)))
    ] + [own(c) for c in range(parts)]
    for load in loads:
        load.start()

    def going(b):
        some = pl.ds(b * batch * cap, batch * cap)
        few = pl.ds((b * batch) ^ (right_mask // batch * batch), batch)
        return (
            pltpu.make_async_copy(halves.at[some], half.at[some], left.at[0, b]),
            pltpu.make_async_copy(energies.at[some], energy.at[some], left.at[1, b]),
            pltpu.make_async_copy(rights.at[few], right.at[few], left.at[2, b]),
        )

    held[orb_dev, :AUXBLK, :] = jnp.zeros((AUXBLK, width), jnp.bfloat16)

    def turn_over(b, carry):
        for u in range(batch):
            turned_over[b * batch + u] = came[b * batch + u, :fit_rows, :].T
        return carry

    lax.fori_loop(0, steps // batch, turn_over, 0)
    for load in loads:
        load.wait()

    def shifted(place):
        moved = []
        for block in range(block_count):
            source = block - shift[place]
            inside = (source >= 0) & (source < block_count)
            slot = jnp.where(inside, first[place], orb_dev)
            begin = pl.multiple_of(jnp.where(inside, source, 0) * AUXBLK, AUXBLK)
            moved.append(held[slot, pl.ds(begin, AUXBLK), :])
        return jnp.concatenate(moved, axis=0)

    def one_batch(b, carry):
        group = [b * batch + u for u in range(batch)]
        couplings, far = [], []
        for step in group:
            side = jnp.concatenate([shifted(step * cap + k) for k in range(cap)], axis=1)
            couplings.append(f32_dot(turned_over[step ^ mask], side, ((1,), (0,))))
            row = came[step ^ mask, fit_rows:, :].astype(jnp.float32)[:1, :]
            far.append(jnp.broadcast_to(row, (width, width)).T)
        for u, step in enumerate(group):
            sides = []
            for k in range(cap):
                place = step * cap + k
                coupling = couplings[u][:, k * width : (k + 1) * width]
                amplitude = coupling / (far[u] + (rows[first[place]] - occupied[place]))
                energies[place] = jnp.sum(coupling * amplitude, axis=0, keepdims=True)
                sides.append(amplitude.astype(jnp.bfloat16))
                halves[place] = sides[-1]
            side = jnp.concatenate(sides, axis=1)
            density = f32_dot(side, side, ((1,), (1,)))
            rights[step ^ right_mask] = fold_symmetric(density).astype(jnp.bfloat16)
        for copy in going(b):
            copy.start()
        return carry

    def finish(b, carry):
        for copy in going(b):
            copy.wait()
        return carry

    lax.fori_loop(0, steps // batch, one_batch, 0)
    lax.fori_loop(0, steps // batch, finish, 0)


def pair_terms(
    mask, right_mask, first, shift, occupied, rows, held, messages, batch=8, parts=8
):
    steps, height, width = messages.shape
    pair_dev = first.shape[0]
    cap = pair_dev // steps
    orb_dev = held.shape[0]
    fit_rows = height - ENERGY_ROWS
    half = (pair_dev, width, width)
    energy = (pair_dev, 1, width)
    right = (steps, width // 2 + DIAGONAL_ROWS, width)
    return pl.pallas_call(
        functools.partial(pairs_kernel, cap, batch, parts, mask, right_mask),
        in_specs=[ANY()] * 5 + [VMEM()],
        out_specs=(ANY(), ANY(), ANY()),
        out_shape=(
            pltpu.HBM(half, jnp.bfloat16),
            pltpu.HBM(energy, jnp.float32),
            pltpu.HBM(right, jnp.bfloat16),
        ),
        scratch_shapes=[
            pltpu.SMEM(first.shape, jnp.int32),
            pltpu.SMEM(shift.shape, jnp.int32),
            pltpu.SMEM(occupied.shape, jnp.float32),
            pltpu.VMEM(rows.shape, jnp.float32),
            pltpu.VMEM((orb_dev + 1, fit_rows, width), jnp.bfloat16),
            pltpu.VMEM((steps, width, fit_rows), jnp.bfloat16),
            pltpu.VMEM(half, jnp.bfloat16),
            pltpu.VMEM(energy, jnp.float32),
            pltpu.VMEM(right, jnp.bfloat16),
            pltpu.SemaphoreType.DMA((4 + parts,)),
            pltpu.SemaphoreType.DMA((3, steps // batch)),
        ],
        compiler_params=pltpu.CompilerParams(vmem_limit_bytes=24 * MIB),
        name="pair_terms",
    )(*map(in_hbm, (first, shift, occupied, rows, held)), messages)


def left_kernel(
    batch, index, first, half, energy, transforms, density, pair_energy, halves, turns, inner, scattered, arrived
):
    orb_dev, width, _ = inner.shape
    pair_dev = half.shape[0]
    loads = [
        pltpu.make_async_copy(half, halves, arrived.at[0]),
        pltpu.make_async_copy(transforms, turns, arrived.at[1]),
    ]
    for load in loads:
        load.start()
    inner[...] = jnp.zeros_like(inner)
    for load in loads:
        load.wait()

    def some_pairs(b, carry):
        places = [b * batch + u for u in range(batch)]
        sums = [f32_dot(halves[place], halves[place], ((0,), (0,))) for place in places]
        for place, one in zip(places, sums):
            slot = first[place]
            inner[slot] = inner[slot] + one
            scattered[index[place]] = energy[place]
        return carry

    lax.fori_loop(0, pair_dev // batch, some_pairs, 0)

    def some_slots(b, carry):
        slots = [b * batch + u for u in range(batch)]
        half_way = [turned(turns[slot], inner[slot]) for slot in slots]
        for slot, one in zip(slots, half_way):
            density[slot] = turned_back(one, turns[slot])
        return carry

    lax.fori_loop(0, orb_dev // batch, some_slots, 0)
    gathered = scattered[...].reshape(pair_dev, width)
    pair_energy[...] = -jnp.sum(gathered.T, axis=0, keepdims=True) / width


def left_density(index, first, half, energy, transforms, batch=8):
    orb_dev = transforms.shape[0]
    pair_dev, width, _ = half.shape
    return pl.pallas_call(
        functools.partial(left_kernel, batch),
        in_specs=[SMEM(), SMEM(), ANY(), VMEM(), ANY()],
        out_specs=(VMEM(), VMEM()),
        out_shape=(
            pltpu.HBM((orb_dev, width, width), jnp.float32),
            pltpu.HBM((1, pair_dev), jnp.float32),
        ),
        scratch_shapes=[
            pltpu.VMEM(half.shape, jnp.bfloat16),
            pltpu.VMEM(transforms.shape, jnp.bfloat16),
            pltpu.VMEM((orb_dev, width, width), jnp.float32),
            pltpu.VMEM((pair_dev, 1, width), jnp.float32),
            pltpu.SemaphoreType.DMA((2,)),
        ],
        compiler_params=pltpu.CompilerParams(vmem_limit_bytes=16 * MIB),
        name="left_density",
    )(*map(in_hbm, (index, first, half, energy, transforms)))


def right_kernel(
    batch, asked_mask, mask, wanted, before, rights, transforms, out, asked, total, parts, turns, arrived, left
):
    senders = rights.shape[0]
    which = pltpu.make_async_copy(wanted, asked, arrived.at[0])
    turns_load = pltpu.make_async_copy(transforms, turns, arrived.at[1])
    total_load = pltpu.make_async_copy(before, total, arrived.at[2])
    for load in (which, turns_load, total_load):
        load.start()

    def unfold(b, carry):
        for u in range(batch):
            full = unfold_symmetric(rights[b * batch + u].astype(jnp.float32))
            parts[b * batch + u] = full.astype(jnp.bfloat16)
        return carry

    lax.fori_loop(0, senders // batch, unfold, 0)
    which.wait()
    turns_load.wait()
    total_load.wait()

    def some_messages(b, carry):
        places = [b * batch + u for u in range(batch)]
        slots = [asked[place ^ mask ^ asked_mask, 0, 0] for place in places]
        half_way = [
            f32_dot(turns[slot], parts[place], ((1,), (0,))) for slot, place in zip(slots, places)
        ]
        sums = [turned_back(one, turns[slot]) for slot, one in zip(slots, half_way)]
        for slot, one in zip(slots, sums):
            total[slot] = total[slot] + one
        return carry

    lax.fori_loop(0, senders // batch, some_messages, 0)

    def going(c):
        slots = pl.ds(c * batch, batch)
        return pltpu.make_async_copy(total.at[slots], out.at[slots], left.at[c])

    for c in range(total.shape[0] // batch):
        going(c).start()
    for c in range(total.shape[0] // batch):
        going(c).wait()


def add_right_density(asked_mask, mask, asked, density, right, transforms, batch=8):
    return pl.pallas_call(
        functools.partial(right_kernel, batch, asked_mask, mask),
        in_specs=[ANY(), ANY(), VMEM(), ANY()],
        out_specs=ANY(),
        out_shape=pltpu.HBM(density.shape, jnp.float32),
        scratch_shapes=[
            pltpu.SMEM(asked.shape, jnp.int32),
            pltpu.VMEM(density.shape, jnp.float32),
            pltpu.VMEM((right.shape[0],) + density.shape[1:], jnp.bfloat16),
            pltpu.VMEM(transforms.shape, jnp.bfloat16),
            pltpu.SemaphoreType.DMA((3,)),
            pltpu.SemaphoreType.DMA((density.shape[0] // batch,)),
        ],
        compiler_params=pltpu.CompilerParams(vmem_limit_bytes=16 * MIB),
        name="add_right_density",
    )(asked, in_hbm(density), right, in_hbm(transforms))


def exchange(messages, mask):
    groups = [[place ^ mask for place in range(messages.shape[0])]]
    return lax.all_to_all(
        messages, "orb", split_axis=0, concat_axis=0, tiled=True, axis_index_groups=groups
    )


def local(pair_list, orbital_slot, blocks, transforms, domain, eps_virt, eps_occ, offsets):
    owners = lax.axis_size("orb")
    orb_dev = blocks.shape[0]
    ask, send, give_back = 3 * owners // 4, owners // 2, 3 * owners // 4
    asked = exchange(wanted_slots(owners, orb_dev, ask, pair_list, orbital_slot), ask)
    rows, held = own_rotated(domain, eps_virt, blocks, transforms)
    incoming = exchange(pack_messages(ask, send, asked, held), send)
    index, first, shift, occupied = plan(
        owners, orb_dev, pair_list, orbital_slot, offsets, eps_occ
    )
    half, energy, right = pair_terms(
        send, give_back, first, shift, occupied, rows, held, incoming
    )
    came_back = exchange(right, give_back)
    density, pair_energy = left_density(index, first, half, energy, transforms)
    density = add_right_density(ask, give_back, asked, density, came_back, transforms)
    return (pair_energy.reshape(-1), density)


def solution(mesh):
    in_specs = (
        P(("groups", "orb"), None),
        P("groups"),
        P(("groups", "orb"), None, None),
        P(("groups", "orb"), None, None),
        P(("groups", "orb"), None),
        P("groups"),
        P("groups"),
        P("groups"),
    )
    out_specs = (P(("groups", "orb")), P(("groups", "orb"), None, None))
    return jax.shard_map(local, mesh=mesh, in_specs=in_specs, out_specs=out_specs, check_vma=False)
```

time: 103 us -> 97.2 us (0.944)
  waiting for transfers between devices: 45.9 us -> 38.4 us
  starting transfers between devices: 22.6 us -> 26.6 us
  local copies, waits for them, and re-layouts: 2.19 us -> 0 us
    all_to_all x3, waiting for transfers between devices: 45.9 us -> 38.4 us  [exchange(): lax.all_to_all(messages, 'orb', split_axis=0, concat_axis=0, tiled=True,...]
    all_to_all x3, starting transfers between devices: 22.6 us -> 26.6 us  [exchange(): lax.all_to_all(messages, 'orb', split_axis=0, concat_axis=0, tiled=True,...]
    unnamed x2 -> x0, local copies, waits for them, and re-layouts: 2.19 us -> none
  transfers between devices with their start and end apart: 3 -> 3, of which waited for: 3 -> 2; matrix products, arithmetic and copies ran while one was open for 0% -> 0% of each run, Pallas kernels for 13% -> 16%
where the time goes in v3:
time: 97.2 us; the launch traced here: 96.5 us
  waiting for transfers between devices  38.4 us (40%)
  Pallas kernels  30.8 us (32%)
  starting transfers between devices  26.6 us (27%)
    all_to_all x3, waiting for transfers between devices, exchange(): lax.all_to_all(messages, 'orb', split_axis=0, concat_axis=0, tiled=True,...  38.4 us
    all_to_all x3, starting transfers between devices, exchange(): lax.all_to_all(messages, 'orb', split_axis=0, concat_axis=0, tiled=True,...  26.6 us
    pallas_call x1, Pallas kernels, left_density(): pl.pallas_call(functools.partial(left_kernel, batch), in_specs=[SMEM(), S...  7.88 us
    pallas_call x1, Pallas kernels, own_rotated(): pl.pallas_call(functools.partial(own_kernel, chunk), in_specs=[VMEM(), VM...  5.7 us
    pallas_call x1, Pallas kernels, pair_terms(): pl.pallas_call(functools.partial(pairs_kernel, cap, batch, parts, mask, r...  5.63 us
    pallas_call x1, Pallas kernels, add_right_density(): pl.pallas_call(functools.partial(right_kernel, batch, asked_mask, mask),...  4.13 us
    pallas_call x1, Pallas kernels, pack_messages(): pl.pallas_call(functools.partial(pack_kernel, asked_mask, mask), in_specs...  3.69 us
    pallas_call x1, Pallas kernels, plan(): pl.pallas_call(functools.partial(plan_kernel, orb_dev, cap), out_shape=(s...  2.08 us
  transfers between devices with their start and end apart: 3, of which 2 were waited for; matrix products, arithmetic and copies ran while one was open for 0% of the time, Pallas kernels for 16%

profile of v3, /device:TPU:0, one launch (start us, length us, event | category | flops | bytes accessed | tf_op | source)
XLA Modules:
  0.0 96.5 jit_solution(3544201082531516755)
XLA Ops:
  0.6 1.6 %wanted_slots.1 = s32[16,1,128]{2,1,0:T(1,128)} custom-call(s32[2,64]{1,0:T(2,128)} %bitcast.4, s32[512]{0:T(512)} %slots.3), custom_call_target="tpu_custom_call" | custom-call | tf_op jit(solution)/shard_map/wanted_slots/pallas_call | solution.py:57
  2.3 8.4 %all-to-all-start = ((s32[16,1,128]{2,1,0:T(1,128)}), s32[16,1,128]{2,1,0:T(1,128)S(1)}, u32[]{:S(2)}, u32[]{:S(2)}) async-start(s32[16,1,128]{2,1,0:T(1,128)} %wanted_slots.1), calls=%async_computation | async-start | bytes 16384 | tf_op jit(solution)/shard_map/all_to_all | solution.py:501
  10.7 5.7 %own_rotated.1 = (f32[32,1,128]{2,1,0:T(1,128)}, bf16[32,528,128]{2,1,0:T(8,128)(2,1)}) custom-call(s32[32,128]{1,0:T(8,128)} %domain.1, f32[16,128]{1,0:T(8,128)} %bitcast.3, bf16[32,512,128]{2,1,0:T(8,128)(2,1)} %blocks.1, bf16[32,128,128]{2,1,0:T(8,128)(2,1)} %transforms.5), custom_call_target="tpu_custom_call" | custom-call | tf_op jit(solution)/shard_map/own_rotated/pallas_call | solution.py:161
  16.4 0.0 all-to-all-done.asked.wanted
  16.4 3.7 %pack_messages.1 = bf16[16,528,128]{2,1,0:T(8,128)(2,1)} custom-call(s32[16,1,128]{2,1,0:T(1,128)S(1)} %all-to-all-done.asked.wanted, bf16[32,528,128]{2,1,0:T(8,128)(2,1)} %get-tuple-element.18.held.refs_4_), custom_call_target="tpu_custom_call" | custom-call | tf_op jit(solution)/shard_map/pack_messages/pallas_call | solution.py:211
  20.1 4.9 %all-to-all-start.1 = ((bf16[16,528,128]{2,1,0:T(8,128)(2,1)}), bf16[16,528,128]{2,1,0:T(8,128)(2,1)S(1)}, u32[]{:S(2)}, u32[]{:S(2)}) async-start(bf16[16,528,128]{2,1,0:T(8,128)(2,1)} %pack_messages.1), calls=%async_computation.1 | async-start | bytes 4325376 | tf_op jit(solution)/shard_map/all_to_all | solution.py:501
  24.9 2.1 %plan.1 = (s32[64]{0:T(128)}, s32[64]{0:T(128)}, s32[64]{0:T(128)}, f32[64]{0:T(128)}) custom-call(s32[2,64]{1,0:T(2,128)} %bitcast.5, s32[512]{0:T(512)} %slots.3, s32[512]{0:T(512)} %offsets.1, f32[512]{0:T(512)} %eps_occ.1), custom_call_target="tpu_custom_call" | custom-call | tf_op jit(solution)/shard_map/plan/pallas_call | solution.py:95
  27.0 37.8 %all-to-all-done.1.refs_5_ = bf16[16,528,128]{2,1,0:T(8,128)(2,1)S(1)} async-done(((bf16[16,528,128]{2,1,0:T(8,128)(2,1)}), bf16[16,528,128]{2,1,0:T(8,128)(2,1)S(1)}, u32[]{:S(2)}, u32[]{:S(2)}) %all-to-all-start.1) | async-done | bytes 2162720 | tf_op jit(solution)/shard_map/all_to_all | solution.py:501
  64.9 5.6 %pair_terms.1 = (bf16[64,128,128]{2,1,0:T(8,128)(2,1)}, f32[64,1,128]{2,1,0:T(1,128)}, bf16[16,80,128]{2,1,0:T(8,128)(2,1)}) custom-call(s32[64]{0:T(128)} %get-tuple-element.14.refs_0_.first, s32[64]{0:T(128)} %get-tuple-element.15.refs_1_, f32[64]{0:T(128)} %get-tuple-element.16.refs_2_, f32[32,1,128]{2,1,0:T(1,128)} %get-tuple-element.17.refs_3_, ...), custom_call_target="tpu_custom_call" | custom-call | tf_op jit(solution)/shard_map/pair_terms/pallas_call | solution.py:348
  70.5 13.4 %all-to-all-start.2 = ((bf16[16,80,128]{2,1,0:T(8,128)(2,1)}), bf16[16,80,128]{2,1,0:T(8,128)(2,1)S(1)}, u32[]{:S(2)}, u32[]{:S(2)}) async-start(bf16[16,80,128]{2,1,0:T(8,128)(2,1)} %get-tuple-element.23), calls=%async_computation.2 | async-start | bytes 655360 | tf_op jit(solution)/shard_map/all_to_all | solution.py:501
  83.9 7.9 %left_density.1 = (f32[32,128,128]{2,1,0:T(8,128)}, f32[1,64]{1,0:T(1,128)}) custom-call(s32[64]{0:T(128)} %get-tuple-element.13.index, s32[64]{0:T(128)} %get-tuple-element.14.refs_0_.first, bf16[64,128,128]{2,1,0:T(8,128)(2,1)} %get-tuple-element.19.half, f32[64,1,128]{2,1,0:T(1,128)} %get-tuple-element.20.energy, bf16[32,128,128]{2,1,0:T(8,128)(2,1)} %transforms.5), custom_call_target="tpu_custom_call" | custom-call | tf_op jit(solution)/shard_map/left_density/pallas_call | solution.py:416
  91.8 0.6 all-to-all-done.2.rights
  92.4 4.1 %add_right_density.1 = f32[32,128,128]{2,1,0:T(8,128)} custom-call(s32[16,1,128]{2,1,0:T(1,128)S(1)} %all-to-all-done.asked.wanted, f32[32,128,128]{2,1,0:T(8,128)} %get-tuple-element.22.before, bf16[16,80,128]{2,1,0:T(8,128)(2,1)S(1)} %all-to-all-done.2.rights, bf16[32,128,128]{2,1,0:T(8,128)(2,1)} %transforms.5), custom_call_target="tpu_custom_call" | custom-call | tf_op jit(solution)/shard_map/add_right_density/pallas_call | solution.py:481
Async XLA Ops:
  2.3 14.1 %all-to-all-start = ((s32[16,1,128]{2,1,0:T(1,128)}), s32[16,1,128]{2,1,0:T(1,128)S(1)}, u32[]{:S(2)}, u32[]{:S(2)}) async-start(s32[16,1,128]{2,1,0:T(1,128)} %wanted_slots.1), calls=%async_computation | async-start | bytes 16384 | tf_op jit(solution)/shard_map/all_to_all | solution.py:501
  20.1 44.8 %all-to-all-start.1 = ((bf16[16,528,128]{2,1,0:T(8,128)(2,1)}), bf16[16,528,128]{2,1,0:T(8,128)(2,1)S(1)}, u32[]{:S(2)}, u32[]{:S(2)}) async-start(bf16[16,528,128]{2,1,0:T(8,128)(2,1)} %pack_messages.1), calls=%async_computation.1 | async-start | bytes 4325376 | tf_op jit(solution)/shard_map/all_to_all | solution.py:501
  70.5 21.9 %all-to-all-start.2 = ((bf16[16,80,128]{2,1,0:T(8,128)(2,1)}), bf16[16,80,128]{2,1,0:T(8,128)(2,1)S(1)}, u32[]{:S(2)}, u32[]{:S(2)}) async-start(bf16[16,80,128]{2,1,0:T(8,128)(2,1)} %get-tuple-element.23), calls=%async_computation.2 | async-start | bytes 655360 | tf_op jit(solution)/shard_map/all_to_all | solution.py:501

commit v4 on v3

--- a/solution.py
+++ b/solution.py
@@ -108,7 +108,7 @@
 
 
 def own_kernel(
-    chunk, domain, eps_virt, blocks, transforms, rows, held, block_rows, turns, made, arrived, left
+    chunk, domain, eps_virt, blocks, transforms, rows, held, wanted, table, found, block_rows, turns, made, arrived, left
 ):
     orb_dev, fit_rows, width = blocks.shape
     chunks = orb_dev // chunk
@@ -124,21 +124,30 @@
         part = pl.ds(c * chunk, chunk)
         return pltpu.make_async_copy(made.at[part], held.at[part], left.at[c])
 
+    loads = [
+        pltpu.make_async_copy(domain, wanted, arrived.at[0, chunks]),
+        pltpu.make_async_copy(eps_virt, table, arrived.at[1, chunks]),
+    ]
+    for load in loads:
+        load.start()
     for c in range(chunks):
         for copy in coming(c):
             copy.start()
-    wanted = domain[...]
-    line, lane = wanted // 128, wanted % 128
-    found = jnp.zeros((orb_dev, width), jnp.float32)
-    for k in range(eps_virt.shape[0]):
-        spread = jnp.broadcast_to(eps_virt[pl.ds(k, 1), :], (orb_dev, width))
+    for load in loads:
+        load.wait()
+    line, lane = wanted[...] // 128, wanted[...] % 128
+    energies = jnp.zeros((orb_dev, width), jnp.float32)
+    for k in range(table.shape[0]):
+        spread = jnp.broadcast_to(table[pl.ds(k, 1), :], (orb_dev, width))
         picked = jnp.take_along_axis(spread, lane, axis=1)
-        found = jnp.where(line == k, picked, found)
-    rounded = found.astype(jnp.bfloat16).astype(jnp.float32)
+        energies = jnp.where(line == k, picked, energies)
+    rounded = energies.astype(jnp.bfloat16).astype(jnp.float32)
     for s in range(orb_dev):
         row = rounded[s : s + 1, :]
-        rows[s] = row
+        found[s] = row
         made[s, fit_rows:, :] = jnp.broadcast_to(row, (ENERGY_ROWS, width)).astype(jnp.bfloat16)
+    rows_out = pltpu.make_async_copy(found, rows, left.at[chunks])
+    rows_out.start()
 
     def one_chunk(c, carry):
         for copy in coming(c):
@@ -151,6 +160,7 @@
         return carry
 
     lax.fori_loop(0, chunks, one_chunk, 0)
+    rows_out.wait()
     for c in range(chunks):
         going(c).wait()
 
@@ -158,24 +168,28 @@
 def own_rotated(domain, eps_virt, blocks, transforms, chunk=4):
     orb_dev, fit_rows, width = blocks.shape
     shape = (orb_dev, fit_rows + ENERGY_ROWS, width)
+    table = (eps_virt.shape[0] // 128, 128)
     return pl.pallas_call(
         functools.partial(own_kernel, chunk),
-        in_specs=[VMEM(), VMEM(), ANY(), ANY()],
-        out_specs=(VMEM(), ANY()),
+        in_specs=[ANY()] * 4,
+        out_specs=(ANY(), ANY()),
         out_shape=(
             pltpu.HBM((orb_dev, 1, width), jnp.float32),
             pltpu.HBM(shape, jnp.bfloat16),
         ),
         scratch_shapes=[
+            pltpu.VMEM(domain.shape, jnp.int32),
+            pltpu.VMEM(table, jnp.float32),
+            pltpu.VMEM((orb_dev, 1, width), jnp.float32),
             pltpu.VMEM(blocks.shape, jnp.bfloat16),
             pltpu.VMEM(transforms.shape, jnp.bfloat16),
             pltpu.VMEM(shape, jnp.bfloat16),
-            pltpu.SemaphoreType.DMA((2, orb_dev // chunk)),
-            pltpu.SemaphoreType.DMA((orb_dev // chunk,)),
+            pltpu.SemaphoreType.DMA((2, orb_dev // chunk + 1)),
+            pltpu.SemaphoreType.DMA((orb_dev // chunk + 1,)),
         ],
         compiler_params=pltpu.CompilerParams(vmem_limit_bytes=16 * MIB),
         name="own_rotated",
-    )(*map(in_hbm, (domain, eps_virt.reshape(-1, 128), blocks, transforms)))
+    )(*map(in_hbm, (domain, eps_virt.reshape(table), blocks, transforms)))
 
 
 def pack_kernel(asked_mask, mask, asked, held, messages, made, arrived, left):
@@ -372,93 +386,129 @@
     )(*map(in_hbm, (first, shift, occupied, rows, held)), messages)
 
 
-def left_kernel(
-    batch, index, first, half, energy, transforms, density, pair_energy, halves, turns, inner, scattered, arrived
-):
+def left_kernel(batch, *refs):
+    inputs, (density, pair_energy), scratch = refs[:5], refs[5:7], refs[7:]
+    index, first, energy, halves, turns, inner, scattered, made, energies, arrived, left = scratch
     orb_dev, width, _ = inner.shape
-    pair_dev = half.shape[0]
+    pair_dev = halves.shape[0]
+    parts = pair_dev // batch
+
+    def half(b):
+        some = pl.ds(b * batch, batch)
+        return pltpu.make_async_copy(inputs[3].at[some], halves.at[some], arrived.at[4 + b])
+
+    def going(b):
+        some = pl.ds(b * batch, batch)
+        return pltpu.make_async_copy(made.at[some], density.at[some], left.at[b])
+
     loads = [
-        pltpu.make_async_copy(half, halves, arrived.at[0]),
-        pltpu.make_async_copy(transforms, turns, arrived.at[1]),
+        pltpu.make_async_copy(inputs[n], target, arrived.at[n])
+        for n, target in enumerate((index, first, energy))
     ]
+    turns_load = pltpu.make_async_copy(inputs[4], turns, arrived.at[3])
     for load in loads:
         load.start()
+    for b in range(parts):
+        half(b).start()
+    turns_load.start()
     inner[...] = jnp.zeros_like(inner)
     for load in loads:
         load.wait()
 
+    def scatter(place, carry):
+        scattered[index[place]] = energy[place]
+        return carry
+
+    lax.fori_loop(0, pair_dev, scatter, 0, unroll=8)
+    gathered = scattered[...].reshape(pair_dev, width)
+    energies[...] = -jnp.sum(gathered.T, axis=0, keepdims=True) / width
+    energies_out = pltpu.make_async_copy(energies, pair_energy, left.at[orb_dev // batch])
+    energies_out.start()
+
     def some_pairs(b, carry):
+        half(b).wait()
         places = [b * batch + u for u in range(batch)]
         sums = [f32_dot(halves[place], halves[place], ((0,), (0,))) for place in places]
         for place, one in zip(places, sums):
             slot = first[place]
             inner[slot] = inner[slot] + one
-            scattered[index[place]] = energy[place]
-        return carry
-
-    lax.fori_loop(0, pair_dev // batch, some_pairs, 0)
+        return carry
+
+    lax.fori_loop(0, parts, some_pairs, 0)
+    turns_load.wait()
 
     def some_slots(b, carry):
         slots = [b * batch + u for u in range(batch)]
         half_way = [turned(turns[slot], inner[slot]) for slot in slots]
         for slot, one in zip(slots, half_way):
-            density[slot] = turned_back(one, turns[slot])
+            made[slot] = turned_back(one, turns[slot])
+        going(b).start()
         return carry
 
     lax.fori_loop(0, orb_dev // batch, some_slots, 0)
-    gathered = scattered[...].reshape(pair_dev, width)
-    pair_energy[...] = -jnp.sum(gathered.T, axis=0, keepdims=True) / width
-
-
-def left_density(index, first, half, energy, transforms, batch=8):
+    energies_out.wait()
+    for b in range(orb_dev // batch):
+        going(b).wait()
+
+
+def left_density(index, first, energy, half, transforms, batch=8):
     orb_dev = transforms.shape[0]
     pair_dev, width, _ = half.shape
+    density = (orb_dev, width, width)
     return pl.pallas_call(
         functools.partial(left_kernel, batch),
-        in_specs=[SMEM(), SMEM(), ANY(), VMEM(), ANY()],
-        out_specs=(VMEM(), VMEM()),
-        out_shape=(
-            pltpu.HBM((orb_dev, width, width), jnp.float32),
-            pltpu.HBM((1, pair_dev), jnp.float32),
-        ),
+        in_specs=[ANY()] * 5,
+        out_specs=(ANY(), ANY()),
+        out_shape=(pltpu.HBM(density, jnp.float32), pltpu.HBM((1, pair_dev), jnp.float32)),
         scratch_shapes=[
+            pltpu.SMEM(index.shape, jnp.int32),
+            pltpu.SMEM(first.shape, jnp.int32),
+            pltpu.VMEM(energy.shape, jnp.float32),
             pltpu.VMEM(half.shape, jnp.bfloat16),
             pltpu.VMEM(transforms.shape, jnp.bfloat16),
-            pltpu.VMEM((orb_dev, width, width), jnp.float32),
-            pltpu.VMEM((pair_dev, 1, width), jnp.float32),
-            pltpu.SemaphoreType.DMA((2,)),
+            pltpu.VMEM(density, jnp.float32),
+            pltpu.VMEM(energy.shape, jnp.float32),
+            pltpu.VMEM(density, jnp.float32),
+            pltpu.VMEM((1, pair_dev), jnp.float32),
+            pltpu.SemaphoreType.DMA((4 + pair_dev // batch,)),
+            pltpu.SemaphoreType.DMA((orb_dev // batch + 1,)),
         ],
         compiler_params=pltpu.CompilerParams(vmem_limit_bytes=16 * MIB),
         name="left_density",
-    )(*map(in_hbm, (index, first, half, energy, transforms)))
+    )(*map(in_hbm, (index, first, energy, half, transforms)))
 
 
 def right_kernel(
-    batch, asked_mask, mask, wanted, before, rights, transforms, out, asked, total, parts, turns, arrived, left
+    batch, parts, asked_mask, mask, wanted, before, rights, transforms, out, asked, total, unfolded, turns, arrived, left
 ):
     senders = rights.shape[0]
-    which = pltpu.make_async_copy(wanted, asked, arrived.at[0])
-    turns_load = pltpu.make_async_copy(transforms, turns, arrived.at[1])
-    total_load = pltpu.make_async_copy(before, total, arrived.at[2])
-    for load in (which, turns_load, total_load):
+    each = total.shape[0] // parts
+    chunks = [pl.ds(c * each, each) for c in range(parts)]
+    loads = [pltpu.make_async_copy(wanted, asked, arrived.at[0, parts])]
+    for n, (source, target) in enumerate(((transforms, turns), (before, total))):
+        for c, chunk in enumerate(chunks):
+            loads.append(
+                pltpu.make_async_copy(source.at[chunk], target.at[chunk], arrived.at[n, c])
+            )
+    for load in loads:
         load.start()
 
     def unfold(b, carry):
         for u in range(batch):
             full = unfold_symmetric(rights[b * batch + u].astype(jnp.float32))
-            parts[b * batch + u] = full.astype(jnp.bfloat16)
+            unfolded[b * batch + u] = full.astype(jnp.bfloat16)
         return carry
 
     lax.fori_loop(0, senders // batch, unfold, 0)
-    which.wait()
-    turns_load.wait()
-    total_load.wait()
+    for load in loads:
+        load.wait()
 
     def some_messages(b, carry):
         places = [b * batch + u for u in range(batch)]
         slots = [asked[place ^ mask ^ asked_mask, 0, 0] for place in places]
         half_way = [
-            f32_dot(turns[slot], parts[place], ((1,), (0,))) for slot, place in zip(slots, places)
+            f32_dot(turns[slot], unfolded[place], ((1,), (0,)))
+            for slot, place in zip(slots, places)
         ]
         sums = [turned_back(one, turns[slot]) for slot, one in zip(slots, half_way)]
         for slot, one in zip(slots, sums):
@@ -467,19 +517,19 @@
 
     lax.fori_loop(0, senders // batch, some_messages, 0)
 
-    def going(c):
-        slots = pl.ds(c * batch, batch)
-        return pltpu.make_async_copy(total.at[slots], out.at[slots], left.at[c])
-
-    for c in range(total.shape[0] // batch):
-        going(c).start()
-    for c in range(total.shape[0] // batch):
-        going(c).wait()
-
-
-def add_right_density(asked_mask, mask, asked, density, right, transforms, batch=8):
-    return pl.pallas_call(
-        functools.partial(right_kernel, batch, asked_mask, mask),
+    stores = [
+        pltpu.make_async_copy(total.at[chunk], out.at[chunk], left.at[c])
+        for c, chunk in enumerate(chunks)
+    ]
+    for store in stores:
+        store.start()
+    for store in stores:
+        store.wait()
+
+
+def add_right_density(asked_mask, mask, asked, density, right, transforms, batch=16, parts=4):
+    return pl.pallas_call(
+        functools.partial(right_kernel, batch, parts, asked_mask, mask),
         in_specs=[ANY(), ANY(), VMEM(), ANY()],
         out_specs=ANY(),
         out_shape=pltpu.HBM(density.shape, jnp.float32),
@@ -488,8 +538,8 @@
             pltpu.VMEM(density.shape, jnp.float32),
             pltpu.VMEM((right.shape[0],) + density.shape[1:], jnp.bfloat16),
             pltpu.VMEM(transforms.shape, jnp.bfloat16),
-            pltpu.SemaphoreType.DMA((3,)),
-            pltpu.SemaphoreType.DMA((density.shape[0] // batch,)),
+            pltpu.SemaphoreType.DMA((2, parts + 1)),
+            pltpu.SemaphoreType.DMA((parts,)),
         ],
         compiler_params=pltpu.CompilerParams(vmem_limit_bytes=16 * MIB),
         name="add_right_density",
@@ -506,7 +556,7 @@
 def local(pair_list, orbital_slot, blocks, transforms, domain, eps_virt, eps_occ, offsets):
     owners = lax.axis_size("orb")
     orb_dev = blocks.shape[0]
-    ask, send, give_back = 3 * owners // 4, owners // 2, 3 * owners // 4
+    ask, send, give_back = owners // 2, owners // 2, 3 * owners // 4
     asked = exchange(wanted_slots(owners, orb_dev, ask, pair_list, orbital_slot), ask)
     rows, held = own_rotated(domain, eps_virt, blocks, transforms)
     incoming = exchange(pack_messages(ask, send, asked, held), send)
@@ -517,7 +567,7 @@
         send, give_back, first, shift, occupied, rows, held, incoming
     )
     came_back = exchange(right, give_back)
-    density, pair_energy = left_density(index, first, half, energy, transforms)
+    density, pair_energy = left_density(index, first, energy, half, transforms)
     density = add_right_density(ask, give_back, asked, density, came_back, transforms)
     return (pair_energy.reshape(-1), density)
 

time: 97.2 us -> 95.1 us (0.978)
  Pallas kernels: 30.8 us -> 27.2 us
  waiting for transfers between devices: 38.4 us -> 40.5 us
    pallas_call x3, Pallas kernels: 17.7 us -> 14.2 us  [the longest x1 5.81 us: left_density(): pl.pallas_call(functools.partial(left_kernel, batch), in_specs=[ANY()] *...]
    all_to_all x3, waiting for transfers between devices: 38.4 us -> 40.5 us  [exchange(): lax.all_to_all(messages, 'orb', split_axis=0, concat_axis=0, tiled=True,...]
  transfers between devices with their start and end apart: 3 -> 3, of which waited for: 2 -> 2; matrix products, arithmetic and copies ran while one was open for 0% -> 0% of each run, Pallas kernels for 16% -> 13%
where the time goes in v4:
time: 95.1 us; the launch traced here: 94.9 us
  waiting for transfers between devices  40.5 us (43%)
  Pallas kernels  27.2 us (29%)
  starting transfers between devices  26.5 us (28%)
    all_to_all x3, waiting for transfers between devices, exchange(): lax.all_to_all(messages, 'orb', split_axis=0, concat_axis=0, tiled=True,...  40.5 us
    all_to_all x3, starting transfers between devices, exchange(): lax.all_to_all(messages, 'orb', split_axis=0, concat_axis=0, tiled=True,...  26.5 us
    pallas_call x1, Pallas kernels, left_density(): pl.pallas_call(functools.partial(left_kernel, batch), in_specs=[ANY()] *...  5.81 us
    pallas_call x1, Pallas kernels, pair_terms(): pl.pallas_call(functools.partial(pairs_kernel, cap, batch, parts, mask, r...  5.64 us
    pallas_call x1, Pallas kernels, own_rotated(): pl.pallas_call(functools.partial(own_kernel, chunk), in_specs=[ANY()] * 4...  4.44 us
    pallas_call x1, Pallas kernels, add_right_density(): pl.pallas_call(functools.partial(right_kernel, batch, parts, asked_mask,...  3.93 us
    pallas_call x1, Pallas kernels, pack_messages(): pl.pallas_call(functools.partial(pack_kernel, asked_mask, mask), in_specs...  3.63 us
    pallas_call x1, Pallas kernels, plan(): pl.pallas_call(functools.partial(plan_kernel, orb_dev, cap), out_shape=(s...  2.08 us
  transfers between devices with their start and end apart: 3, of which 2 were waited for; matrix products, arithmetic and copies ran while one was open for 0% of the time, Pallas kernels for 13%

profile of v4, /device:TPU:0, one launch (start us, length us, event | category | flops | bytes accessed | tf_op | source)
XLA Modules:
  0.0 94.9 jit_solution(7582662723150642562)
XLA Ops:
  0.6 1.6 %wanted_slots.1 = s32[16,1,128]{2,1,0:T(1,128)} custom-call(s32[2,64]{1,0:T(2,128)} %bitcast.4, s32[512]{0:T(512)} %slots.3), custom_call_target="tpu_custom_call" | custom-call | tf_op jit(solution)/shard_map/wanted_slots/pallas_call | solution.py:57
  2.3 7.9 %all-to-all-start = ((s32[16,1,128]{2,1,0:T(1,128)}), s32[16,1,128]{2,1,0:T(1,128)S(1)}, u32[]{:S(2)}, u32[]{:S(2)}) async-start(s32[16,1,128]{2,1,0:T(1,128)} %wanted_slots.1), calls=%async_computation | async-start | bytes 16384 | tf_op jit(solution)/shard_map/all_to_all | solution.py:551
  10.1 4.4 %own_rotated.1 = (f32[32,1,128]{2,1,0:T(1,128)}, bf16[32,528,128]{2,1,0:T(8,128)(2,1)}) custom-call(s32[32,128]{1,0:T(8,128)} %domain.1, f32[16,128]{1,0:T(8,128)} %bitcast.3, bf16[32,512,128]{2,1,0:T(8,128)(2,1)} %blocks.1, bf16[32,128,128]{2,1,0:T(8,128)(2,1)} %transforms.3), custom_call_target="tpu_custom_call" | custom-call | tf_op jit(solution)/shard_map/own_rotated/pallas_call | solution.py:172
  14.6 0.0 all-to-all-done.asked.wanted
  14.6 3.6 %pack_messages.1 = bf16[16,528,128]{2,1,0:T(8,128)(2,1)} custom-call(s32[16,1,128]{2,1,0:T(1,128)S(1)} %all-to-all-done.asked.wanted, bf16[32,528,128]{2,1,0:T(8,128)(2,1)} %get-tuple-element.18.held.refs_4_), custom_call_target="tpu_custom_call" | custom-call | tf_op jit(solution)/shard_map/pack_messages/pallas_call | solution.py:225
  18.2 5.3 %all-to-all-start.1 = ((bf16[16,528,128]{2,1,0:T(8,128)(2,1)}), bf16[16,528,128]{2,1,0:T(8,128)(2,1)S(1)}, u32[]{:S(2)}, u32[]{:S(2)}) async-start(bf16[16,528,128]{2,1,0:T(8,128)(2,1)} %pack_messages.1), calls=%async_computation.1 | async-start | bytes 4325376 | tf_op jit(solution)/shard_map/all_to_all | solution.py:551
  23.5 2.1 %plan.1 = (s32[64]{0:T(128)}, s32[64]{0:T(128)}, s32[64]{0:T(128)}, f32[64]{0:T(128)}) custom-call(s32[2,64]{1,0:T(2,128)} %bitcast.5, s32[512]{0:T(512)} %slots.3, s32[512]{0:T(512)} %offsets.1, f32[512]{0:T(512)} %eps_occ.1), custom_call_target="tpu_custom_call" | custom-call | tf_op jit(solution)/shard_map/plan/pallas_call | solution.py:95
  25.6 37.8 %all-to-all-done.1.refs_5_ = bf16[16,528,128]{2,1,0:T(8,128)(2,1)S(1)} async-done(((bf16[16,528,128]{2,1,0:T(8,128)(2,1)}), bf16[16,528,128]{2,1,0:T(8,128)(2,1)S(1)}, u32[]{:S(2)}, u32[]{:S(2)}) %all-to-all-start.1) | async-done | bytes 2162720 | tf_op jit(solution)/shard_map/all_to_all | solution.py:551
  63.5 5.6 %pair_terms.1 = (bf16[64,128,128]{2,1,0:T(8,128)(2,1)}, f32[64,1,128]{2,1,0:T(1,128)}, bf16[16,80,128]{2,1,0:T(8,128)(2,1)}) custom-call(s32[64]{0:T(128)} %get-tuple-element.14.refs_0_.refs_1_, s32[64]{0:T(128)} %get-tuple-element.15.refs_1_, f32[64]{0:T(128)} %get-tuple-element.16.refs_2_, f32[32,1,128]{2,1,0:T(1,128)} %get-tuple-element.17.refs_3_, ...), custom_call_target="tpu_custom_call" | custom-call | tf_op jit(solution)/shard_map/pair_terms/pallas_call | solution.py:362
  69.1 13.4 %all-to-all-start.2 = ((bf16[16,80,128]{2,1,0:T(8,128)(2,1)}), bf16[16,80,128]{2,1,0:T(8,128)(2,1)S(1)}, u32[]{:S(2)}, u32[]{:S(2)}) async-start(bf16[16,80,128]{2,1,0:T(8,128)(2,1)} %get-tuple-element.23), calls=%async_computation.2 | async-start | bytes 655360 | tf_op jit(solution)/shard_map/all_to_all | solution.py:551
  82.5 5.8 %left_density.1 = (f32[32,128,128]{2,1,0:T(8,128)}, f32[1,64]{1,0:T(1,128)}) custom-call(s32[64]{0:T(128)} %get-tuple-element.13.refs_0_, s32[64]{0:T(128)} %get-tuple-element.14.refs_0_.refs_1_, f32[64,1,128]{2,1,0:T(1,128)} %get-tuple-element.19.refs_2_, bf16[64,128,128]{2,1,0:T(8,128)(2,1)} %get-tuple-element.20.refs_3_, bf16[32,128,128]{2,1,0:T(8,128)(2,1)} %transforms.3), custom_call_target="tpu_custom_call" | custom-call | tf_op jit(solution)/shard_map/left_density/pallas_call | solution.py:458
  88.3 2.7 %all-to-all-done.2.rights = bf16[16,80,128]{2,1,0:T(8,128)(2,1)S(1)} async-done(((bf16[16,80,128]{2,1,0:T(8,128)(2,1)}), bf16[16,80,128]{2,1,0:T(8,128)(2,1)S(1)}, u32[]{:S(2)}, u32[]{:S(2)}) %all-to-all-start.2) | async-done | bytes 327712 | tf_op jit(solution)/shard_map/all_to_all | solution.py:551
  90.9 3.9 %add_right_density.1 = f32[32,128,128]{2,1,0:T(8,128)} custom-call(s32[16,1,128]{2,1,0:T(1,128)S(1)} %all-to-all-done.asked.wanted, f32[32,128,128]{2,1,0:T(8,128)} %get-tuple-element.22.before, bf16[16,80,128]{2,1,0:T(8,128)(2,1)S(1)} %all-to-all-done.2.rights, bf16[32,128,128]{2,1,0:T(8,128)(2,1)} %transforms.3), custom_call_target="tpu_custom_call" | custom-call | tf_op jit(solution)/shard_map/add_right_density/pallas_call | solution.py:531
Async XLA Ops:
  2.3 12.3 %all-to-all-start = ((s32[16,1,128]{2,1,0:T(1,128)}), s32[16,1,128]{2,1,0:T(1,128)S(1)}, u32[]{:S(2)}, u32[]{:S(2)}) async-start(s32[16,1,128]{2,1,0:T(1,128)} %wanted_slots.1), calls=%async_computation | async-start | bytes 16384 | tf_op jit(solution)/shard_map/all_to_all | solution.py:551
  18.2 45.2 %all-to-all-start.1 = ((bf16[16,528,128]{2,1,0:T(8,128)(2,1)}), bf16[16,528,128]{2,1,0:T(8,128)(2,1)S(1)}, u32[]{:S(2)}, u32[]{:S(2)}) async-start(bf16[16,528,128]{2,1,0:T(8,128)(2,1)} %pack_messages.1), calls=%async_computation.1 | async-start | bytes 4325376 | tf_op jit(solution)/shard_map/all_to_all | solution.py:551
  69.1 21.9 %all-to-all-start.2 = ((bf16[16,80,128]{2,1,0:T(8,128)(2,1)}), bf16[16,80,128]{2,1,0:T(8,128)(2,1)S(1)}, u32[]{:S(2)}, u32[]{:S(2)}) async-start(bf16[16,80,128]{2,1,0:T(8,128)(2,1)} %get-tuple-element.23), calls=%async_computation.2 | async-start | bytes 655360 | tf_op jit(solution)/shard_map/all_to_all | solution.py:551

commit v5 on v4

--- a/solution.py
+++ b/solution.py
@@ -556,7 +556,7 @@
 def local(pair_list, orbital_slot, blocks, transforms, domain, eps_virt, eps_occ, offsets):
     owners = lax.axis_size("orb")
     orb_dev = blocks.shape[0]
-    ask, send, give_back = owners // 2, owners // 2, 3 * owners // 4
+    ask, send, give_back = owners // 2, owners // 2 + 1, 3 * owners // 4 + 1
     asked = exchange(wanted_slots(owners, orb_dev, ask, pair_list, orbital_slot), ask)
     rows, held = own_rotated(domain, eps_virt, blocks, transforms)
     incoming = exchange(pack_messages(ask, send, asked, held), send)

time: 95.1 us -> 94.6 us (level)
  no operation moved by 1% of the time
where the time goes in v5:
time: 94.6 us; the launch traced here: 94.2 us
  waiting for transfers between devices  40.3 us (43%)
  Pallas kernels  26.8 us (28%)
  starting transfers between devices  26.4 us (28%)
    all_to_all x3, waiting for transfers between devices, exchange(): lax.all_to_all(messages, 'orb', split_axis=0, concat_axis=0, tiled=True,...  40.3 us
    all_to_all x3, starting transfers between devices, exchange(): lax.all_to_all(messages, 'orb', split_axis=0, concat_axis=0, tiled=True,...  26.4 us
    pallas_call x1, Pallas kernels, left_density(): pl.pallas_call(functools.partial(left_kernel, batch), in_specs=[ANY()] *...  5.82 us
    pallas_call x1, Pallas kernels, pair_terms(): pl.pallas_call(functools.partial(pairs_kernel, cap, batch, parts, mask, r...  5.64 us
    pallas_call x1, Pallas kernels, own_rotated(): pl.pallas_call(functools.partial(own_kernel, chunk), in_specs=[ANY()] * 4...  4.44 us
    pallas_call x1, Pallas kernels, add_right_density(): pl.pallas_call(functools.partial(right_kernel, batch, parts, asked_mask,...  3.93 us
    pallas_call x1, Pallas kernels, pack_messages(): pl.pallas_call(functools.partial(pack_kernel, asked_mask, mask), in_specs...  3.29 us
    pallas_call x1, Pallas kernels, plan(): pl.pallas_call(functools.partial(plan_kernel, orb_dev, cap), out_shape=(s...  2.08 us
  transfers between devices with their start and end apart: 3, of which 2 were waited for; matrix products, arithmetic and copies ran while one was open for 0% of the time, Pallas kernels for 13%

profile of v5, /device:TPU:0, one launch (start us, length us, event | category | flops | bytes accessed | tf_op | source)
XLA Modules:
  0.0 94.2 jit_solution(11097705696818706793)
XLA Ops:
  0.6 1.6 %wanted_slots.1 = s32[16,1,128]{2,1,0:T(1,128)} custom-call(s32[2,64]{1,0:T(2,128)} %bitcast.4, s32[512]{0:T(512)} %slots.3), custom_call_target="tpu_custom_call" | custom-call | tf_op jit(solution)/shard_map/wanted_slots/pallas_call | solution.py:57
  2.3 7.9 %all-to-all-start = ((s32[16,1,128]{2,1,0:T(1,128)}), s32[16,1,128]{2,1,0:T(1,128)S(1)}, u32[]{:S(2)}, u32[]{:S(2)}) async-start(s32[16,1,128]{2,1,0:T(1,128)} %wanted_slots.1), calls=%async_computation | async-start | bytes 16384 | tf_op jit(solution)/shard_map/all_to_all | solution.py:551
  10.1 4.4 %own_rotated.1 = (f32[32,1,128]{2,1,0:T(1,128)}, bf16[32,528,128]{2,1,0:T(8,128)(2,1)}) custom-call(s32[32,128]{1,0:T(8,128)} %domain.1, f32[16,128]{1,0:T(8,128)} %bitcast.3, bf16[32,512,128]{2,1,0:T(8,128)(2,1)} %blocks.1, bf16[32,128,128]{2,1,0:T(8,128)(2,1)} %transforms.3), custom_call_target="tpu_custom_call" | custom-call | tf_op jit(solution)/shard_map/own_rotated/pallas_call | solution.py:172
  14.6 0.0 all-to-all-done.asked.wanted
  14.6 3.3 %pack_messages.1 = bf16[16,528,128]{2,1,0:T(8,128)(2,1)} custom-call(s32[16,1,128]{2,1,0:T(1,128)S(1)} %all-to-all-done.asked.wanted, bf16[32,528,128]{2,1,0:T(8,128)(2,1)} %get-tuple-element.18.held.refs_4_), custom_call_target="tpu_custom_call" | custom-call | tf_op jit(solution)/shard_map/pack_messages/pallas_call | solution.py:225
  17.9 5.3 %all-to-all-start.1 = ((bf16[16,528,128]{2,1,0:T(8,128)(2,1)}), bf16[16,528,128]{2,1,0:T(8,128)(2,1)S(1)}, u32[]{:S(2)}, u32[]{:S(2)}) async-start(bf16[16,528,128]{2,1,0:T(8,128)(2,1)} %pack_messages.1), calls=%async_computation.1 | async-start | bytes 4325376 | tf_op jit(solution)/shard_map/all_to_all | solution.py:551
  23.2 2.1 %plan.1 = (s32[64]{0:T(128)}, s32[64]{0:T(128)}, s32[64]{0:T(128)}, f32[64]{0:T(128)}) custom-call(s32[2,64]{1,0:T(2,128)} %bitcast.5, s32[512]{0:T(512)} %slots.3, s32[512]{0:T(512)} %offsets.1, f32[512]{0:T(512)} %eps_occ.1), custom_call_target="tpu_custom_call" | custom-call | tf_op jit(solution)/shard_map/plan/pallas_call | solution.py:95
  25.3 37.7 %all-to-all-done.1.refs_5_ = bf16[16,528,128]{2,1,0:T(8,128)(2,1)S(1)} async-done(((bf16[16,528,128]{2,1,0:T(8,128)(2,1)}), bf16[16,528,128]{2,1,0:T(8,128)(2,1)S(1)}, u32[]{:S(2)}, u32[]{:S(2)}) %all-to-all-start.1) | async-done | bytes 2162720 | tf_op jit(solution)/shard_map/all_to_all | solution.py:551
  63.0 5.6 %pair_terms.1 = (bf16[64,128,128]{2,1,0:T(8,128)(2,1)}, f32[64,1,128]{2,1,0:T(1,128)}, bf16[16,80,128]{2,1,0:T(8,128)(2,1)}) custom-call(s32[64]{0:T(128)} %get-tuple-element.14.refs_0_.refs_1_, s32[64]{0:T(128)} %get-tuple-element.15.refs_1_, f32[64]{0:T(128)} %get-tuple-element.16.refs_2_, f32[32,1,128]{2,1,0:T(1,128)} %get-tuple-element.17.refs_3_, ...), custom_call_target="tpu_custom_call" | custom-call | tf_op jit(solution)/shard_map/pair_terms/pallas_call | solution.py:362
  68.6 13.2 %all-to-all-start.2 = ((bf16[16,80,128]{2,1,0:T(8,128)(2,1)}), bf16[16,80,128]{2,1,0:T(8,128)(2,1)S(1)}, u32[]{:S(2)}, u32[]{:S(2)}) async-start(bf16[16,80,128]{2,1,0:T(8,128)(2,1)} %get-tuple-element.23), calls=%async_computation.2 | async-start | bytes 655360 | tf_op jit(solution)/shard_map/all_to_all | solution.py:551
  81.8 5.8 %left_density.1 = (f32[32,128,128]{2,1,0:T(8,128)}, f32[1,64]{1,0:T(1,128)}) custom-call(s32[64]{0:T(128)} %get-tuple-element.13.refs_0_, s32[64]{0:T(128)} %get-tuple-element.14.refs_0_.refs_1_, f32[64,1,128]{2,1,0:T(1,128)} %get-tuple-element.19.refs_2_, bf16[64,128,128]{2,1,0:T(8,128)(2,1)} %get-tuple-element.20.refs_3_, bf16[32,128,128]{2,1,0:T(8,128)(2,1)} %transforms.3), custom_call_target="tpu_custom_call" | custom-call | tf_op jit(solution)/shard_map/left_density/pallas_call | solution.py:458
  87.6 2.6 %all-to-all-done.2.rights = bf16[16,80,128]{2,1,0:T(8,128)(2,1)S(1)} async-done(((bf16[16,80,128]{2,1,0:T(8,128)(2,1)}), bf16[16,80,128]{2,1,0:T(8,128)(2,1)S(1)}, u32[]{:S(2)}, u32[]{:S(2)}) %all-to-all-start.2) | async-done | bytes 327712 | tf_op jit(solution)/shard_map/all_to_all | solution.py:551
  90.2 3.9 %add_right_density.1 = f32[32,128,128]{2,1,0:T(8,128)} custom-call(s32[16,1,128]{2,1,0:T(1,128)S(1)} %all-to-all-done.asked.wanted, f32[32,128,128]{2,1,0:T(8,128)} %get-tuple-element.22.before, bf16[16,80,128]{2,1,0:T(8,128)(2,1)S(1)} %all-to-all-done.2.rights, bf16[32,128,128]{2,1,0:T(8,128)(2,1)} %transforms.3), custom_call_target="tpu_custom_call" | custom-call | tf_op jit(solution)/shard_map/add_right_density/pallas_call | solution.py:531
Async XLA Ops:
  2.3 12.3 %all-to-all-start = ((s32[16,1,128]{2,1,0:T(1,128)}), s32[16,1,128]{2,1,0:T(1,128)S(1)}, u32[]{:S(2)}, u32[]{:S(2)}) async-start(s32[16,1,128]{2,1,0:T(1,128)} %wanted_slots.1), calls=%async_computation | async-start | bytes 16384 | tf_op jit(solution)/shard_map/all_to_all | solution.py:551
  17.9 45.1 %all-to-all-start.1 = ((bf16[16,528,128]{2,1,0:T(8,128)(2,1)}), bf16[16,528,128]{2,1,0:T(8,128)(2,1)S(1)}, u32[]{:S(2)}, u32[]{:S(2)}) async-start(bf16[16,528,128]{2,1,0:T(8,128)(2,1)} %pack_messages.1), calls=%async_computation.1 | async-start | bytes 4325376 | tf_op jit(solution)/shard_map/all_to_all | solution.py:551
  68.6 21.6 %all-to-all-start.2 = ((bf16[16,80,128]{2,1,0:T(8,128)(2,1)}), bf16[16,80,128]{2,1,0:T(8,128)(2,1)S(1)}, u32[]{:S(2)}, u32[]{:S(2)}) async-start(bf16[16,80,128]{2,1,0:T(8,128)(2,1)} %get-tuple-element.23), calls=%async_computation.2 | async-start | bytes 655360 | tf_op jit(solution)/shard_map/all_to_all | solution.py:551

commit v6 on v5

--- a/solution.py
+++ b/solution.py
@@ -165,7 +165,7 @@
         going(c).wait()
 
 
-def own_rotated(domain, eps_virt, blocks, transforms, chunk=4):
+def own_rotated(domain, eps_virt, blocks, transforms, chunk=8):
     orb_dev, fit_rows, width = blocks.shape
     shape = (orb_dev, fit_rows + ENERGY_ROWS, width)
     table = (eps_virt.shape[0] // 128, 128)

time: 94.6 us -> 94.3 us (level)
  no operation moved by 1% of the time
where the time goes in v6:
time: 94.3 us; the launch traced here: 93.8 us
  waiting for transfers between devices  40.3 us (43%)
  Pallas kernels  27.1 us (29%)
  starting transfers between devices  25.8 us (27%)
    all_to_all x3, waiting for transfers between devices, exchange(): lax.all_to_all(messages, 'orb', split_axis=0, concat_axis=0, tiled=True,...  40.3 us
    all_to_all x3, starting transfers between devices, exchange(): lax.all_to_all(messages, 'orb', split_axis=0, concat_axis=0, tiled=True,...  25.8 us
    pallas_call x1, Pallas kernels, left_density(): pl.pallas_call(functools.partial(left_kernel, batch), in_specs=[ANY()] *...  5.82 us
    pallas_call x1, Pallas kernels, pair_terms(): pl.pallas_call(functools.partial(pairs_kernel, cap, batch, parts, mask, r...  5.63 us
    pallas_call x1, Pallas kernels, own_rotated(): pl.pallas_call(functools.partial(own_kernel, chunk), in_specs=[ANY()] * 4...  4.14 us
    pallas_call x1, Pallas kernels, add_right_density(): pl.pallas_call(functools.partial(right_kernel, batch, parts, asked_mask,...  3.93 us
    pallas_call x1, Pallas kernels, pack_messages(): pl.pallas_call(functools.partial(pack_kernel, asked_mask, mask), in_specs...  3.88 us
    pallas_call x1, Pallas kernels, plan(): pl.pallas_call(functools.partial(plan_kernel, orb_dev, cap), out_shape=(s...  2.08 us
  transfers between devices with their start and end apart: 3, of which 2 were waited for; matrix products, arithmetic and copies ran while one was open for 0% of the time, Pallas kernels for 13%

profile of v6, /device:TPU:0, one launch (start us, length us, event | category | flops | bytes accessed | tf_op | source)
XLA Modules:
  0.0 93.8 jit_solution(16732415021984890862)
XLA Ops:
  0.6 1.6 %wanted_slots.1 = s32[16,1,128]{2,1,0:T(1,128)} custom-call(s32[2,64]{1,0:T(2,128)} %bitcast.4, s32[512]{0:T(512)} %slots.3), custom_call_target="tpu_custom_call" | custom-call | tf_op jit(solution)/shard_map/wanted_slots/pallas_call | solution.py:57
  2.3 7.9 %all-to-all-start = ((s32[16,1,128]{2,1,0:T(1,128)}), s32[16,1,128]{2,1,0:T(1,128)S(1)}, u32[]{:S(2)}, u32[]{:S(2)}) async-start(s32[16,1,128]{2,1,0:T(1,128)} %wanted_slots.1), calls=%async_computation | async-start | bytes 16384 | tf_op jit(solution)/shard_map/all_to_all | solution.py:551
  10.1 4.1 %own_rotated.1 = (f32[32,1,128]{2,1,0:T(1,128)}, bf16[32,528,128]{2,1,0:T(8,128)(2,1)}) custom-call(s32[32,128]{1,0:T(8,128)} %domain.1, f32[16,128]{1,0:T(8,128)} %bitcast.3, bf16[32,512,128]{2,1,0:T(8,128)(2,1)} %blocks.1, bf16[32,128,128]{2,1,0:T(8,128)(2,1)} %transforms.3), custom_call_target="tpu_custom_call" | custom-call | tf_op jit(solution)/shard_map/own_rotated/pallas_call | solution.py:172
  14.3 0.0 all-to-all-done.asked.wanted
  14.3 3.9 %pack_messages.1 = bf16[16,528,128]{2,1,0:T(8,128)(2,1)} custom-call(s32[16,1,128]{2,1,0:T(1,128)S(1)} %all-to-all-done.asked.wanted, bf16[32,528,128]{2,1,0:T(8,128)(2,1)} %get-tuple-element.18.held.refs_4_), custom_call_target="tpu_custom_call" | custom-call | tf_op jit(solution)/shard_map/pack_messages/pallas_call | solution.py:225
  18.2 4.7 %all-to-all-start.1 = ((bf16[16,528,128]{2,1,0:T(8,128)(2,1)}), bf16[16,528,128]{2,1,0:T(8,128)(2,1)S(1)}, u32[]{:S(2)}, u32[]{:S(2)}) async-start(bf16[16,528,128]{2,1,0:T(8,128)(2,1)} %pack_messages.1), calls=%async_computation.1 | async-start | bytes 4325376 | tf_op jit(solution)/shard_map/all_to_all | solution.py:551
  22.9 2.1 %plan.1 = (s32[64]{0:T(128)}, s32[64]{0:T(128)}, s32[64]{0:T(128)}, f32[64]{0:T(128)}) custom-call(s32[2,64]{1,0:T(2,128)} %bitcast.5, s32[512]{0:T(512)} %slots.3, s32[512]{0:T(512)} %offsets.1, f32[512]{0:T(512)} %eps_occ.1), custom_call_target="tpu_custom_call" | custom-call | tf_op jit(solution)/shard_map/plan/pallas_call | solution.py:95
  25.0 37.7 %all-to-all-done.1.refs_5_ = bf16[16,528,128]{2,1,0:T(8,128)(2,1)S(1)} async-done(((bf16[16,528,128]{2,1,0:T(8,128)(2,1)}), bf16[16,528,128]{2,1,0:T(8,128)(2,1)S(1)}, u32[]{:S(2)}, u32[]{:S(2)}) %all-to-all-start.1) | async-done | bytes 2162720 | tf_op jit(solution)/shard_map/all_to_all | solution.py:551
  62.6 5.6 %pair_terms.1 = (bf16[64,128,128]{2,1,0:T(8,128)(2,1)}, f32[64,1,128]{2,1,0:T(1,128)}, bf16[16,80,128]{2,1,0:T(8,128)(2,1)}) custom-call(s32[64]{0:T(128)} %get-tuple-element.14.refs_0_.refs_1_, s32[64]{0:T(128)} %get-tuple-element.15.refs_1_, f32[64]{0:T(128)} %get-tuple-element.16.refs_2_, f32[32,1,128]{2,1,0:T(1,128)} %get-tuple-element.17.refs_3_, ...), custom_call_target="tpu_custom_call" | custom-call | tf_op jit(solution)/shard_map/pair_terms/pallas_call | solution.py:362
  68.3 13.2 %all-to-all-start.2 = ((bf16[16,80,128]{2,1,0:T(8,128)(2,1)}), bf16[16,80,128]{2,1,0:T(8,128)(2,1)S(1)}, u32[]{:S(2)}, u32[]{:S(2)}) async-start(bf16[16,80,128]{2,1,0:T(8,128)(2,1)} %get-tuple-element.23), calls=%async_computation.2 | async-start | bytes 655360 | tf_op jit(solution)/shard_map/all_to_all | solution.py:551
  81.5 5.8 %left_density.1 = (f32[32,128,128]{2,1,0:T(8,128)}, f32[1,64]{1,0:T(1,128)}) custom-call(s32[64]{0:T(128)} %get-tuple-element.13.refs_0_, s32[64]{0:T(128)} %get-tuple-element.14.refs_0_.refs_1_, f32[64,1,128]{2,1,0:T(1,128)} %get-tuple-element.19.refs_2_, bf16[64,128,128]{2,1,0:T(8,128)(2,1)} %get-tuple-element.20.refs_3_, bf16[32,128,128]{2,1,0:T(8,128)(2,1)} %transforms.3), custom_call_target="tpu_custom_call" | custom-call | tf_op jit(solution)/shard_map/left_density/pallas_call | solution.py:458
  87.3 2.6 %all-to-all-done.2.rights = bf16[16,80,128]{2,1,0:T(8,128)(2,1)S(1)} async-done(((bf16[16,80,128]{2,1,0:T(8,128)(2,1)}), bf16[16,80,128]{2,1,0:T(8,128)(2,1)S(1)}, u32[]{:S(2)}, u32[]{:S(2)}) %all-to-all-start.2) | async-done | bytes 327712 | tf_op jit(solution)/shard_map/all_to_all | solution.py:551
  89.9 3.9 %add_right_density.1 = f32[32,128,128]{2,1,0:T(8,128)} custom-call(s32[16,1,128]{2,1,0:T(1,128)S(1)} %all-to-all-done.asked.wanted, f32[32,128,128]{2,1,0:T(8,128)} %get-tuple-element.22.before, bf16[16,80,128]{2,1,0:T(8,128)(2,1)S(1)} %all-to-all-done.2.rights, bf16[32,128,128]{2,1,0:T(8,128)(2,1)} %transforms.3), custom_call_target="tpu_custom_call" | custom-call | tf_op jit(solution)/shard_map/add_right_density/pallas_call | solution.py:531
Async XLA Ops:
  2.3 12.0 %all-to-all-start = ((s32[16,1,128]{2,1,0:T(1,128)}), s32[16,1,128]{2,1,0:T(1,128)S(1)}, u32[]{:S(2)}, u32[]{:S(2)}) async-start(s32[16,1,128]{2,1,0:T(1,128)} %wanted_slots.1), calls=%async_computation | async-start | bytes 16384 | tf_op jit(solution)/shard_map/all_to_all | solution.py:551
  18.2 44.5 %all-to-all-start.1 = ((bf16[16,528,128]{2,1,0:T(8,128)(2,1)}), bf16[16,528,128]{2,1,0:T(8,128)(2,1)S(1)}, u32[]{:S(2)}, u32[]{:S(2)}) async-start(bf16[16,528,128]{2,1,0:T(8,128)(2,1)} %pack_messages.1), calls=%async_computation.1 | async-start | bytes 4325376 | tf_op jit(solution)/shard_map/all_to_all | solution.py:551
  68.3 21.6 %all-to-all-start.2 = ((bf16[16,80,128]{2,1,0:T(8,128)(2,1)}), bf16[16,80,128]{2,1,0:T(8,128)(2,1)S(1)}, u32[]{:S(2)}, u32[]{:S(2)}) async-start(bf16[16,80,128]{2,1,0:T(8,128)(2,1)} %get-tuple-element.23), calls=%async_computation.2 | async-start | bytes 655360 | tf_op jit(solution)/shard_map/all_to_all | solution.py:551
